TPU v7x, 32 devices: a whole 2x2x4 slice. The times are simulated.
32 devices in a mesh: gx: 8 (over z, y), gy: 4 (over x, core).
Axes of the slice: x: 2, y: 2, z: 4, core: 2. Of those that a mesh axis runs over, the one named last changes fastest.
Arguments:
- snapshot_panel: float32 [64, 65536], P(None, ('gx', 'gy')), may hold values from -2500 to 2500, as said below
- following: float32 [960, 65536], P(None, ('gx', 'gy')), may hold values from -2500 to 2500, as said below
Outputs:
- basis_rows: float32 [64, 65536], P(None, ('gx', 'gy'))
- upper_factor: float32 [64, 64], replicated
- projection: float32 [64, 960], replicated
Inputs may be any that keep to these rules, and one draw needn't show every extreme that they name: `snapshot_panel`: real-valued snapshots of full rank. `following`: real-valued snapshots.
All inputs are finite; a program needn't handle non-finite values.
Results may differ from a plain program's by a relative error of at most 0.000077.
Values sent between devices are 32-bit elements; how exact they have to be, the bound alone decides.
A program may use at most 64 MiB of HBM per device.

v0:
```python
import math

import jax
import jax.numpy as jnp
from jax import lax
from jax.sharding import PartitionSpec as P


def swapped(block, axis, distance):
    count = lax.axis_size(axis)
    route = []
    for low in range(count):
        high = low | 1 << distance
        if high != low and high < count:
            route += [(low, high), (high, low)]
    return lax.ppermute(block, axis, route)


def inner_product(left, right):
    return lax.dot_general(
        left,
        right,
        (((1,), (1,)), ((), ())),
        precision=lax.Precision.HIGHEST,
        preferred_element_type=jnp.float32,
    )


def plain_product(left, right):
    return jnp.dot(left, right, precision=lax.Precision.HIGHEST, preferred_element_type=jnp.float32)


def lower_solve(lower_factor, values):
    return jax.scipy.linalg.solve_triangular(lower_factor, values, lower=True)


def merge_blocks(own_block, their_block, panel_width):
    own_lower = own_block[:, :panel_width]
    their_lower = their_block[:, :panel_width]
    summed_gram = inner_product(own_lower, own_lower) + inner_product(their_lower, their_lower)
    merged_lower = jnp.linalg.cholesky(summed_gram)
    carried = plain_product(own_lower, own_block[:, panel_width:]) + plain_product(
        their_lower, their_block[:, panel_width:]
    )
    return jnp.concatenate([merged_lower, lower_solve(merged_lower, carried)], axis=1)


def body(snapshot_panel, following):
    panel_width = snapshot_panel.shape[0]
    root_rows = math.sqrt(snapshot_panel.shape[1] * lax.axis_size(("gx", "gy")))
    local_lower = jnp.linalg.cholesky(inner_product(snapshot_panel, snapshot_panel))
    carried_block = jnp.concatenate(
        [local_lower, lower_solve(local_lower, inner_product(snapshot_panel, following))], axis=1
    )
    for bit_index in range(lax.axis_size("gx").bit_length() - 1):
        carried_block = merge_blocks(
            carried_block, swapped(carried_block, "gx", bit_index), panel_width
        )
    for bit_index in range(lax.axis_size("gy").bit_length() - 1):
        carried_block = merge_blocks(
            carried_block, swapped(carried_block, "gy", bit_index), panel_width
        )
    lower_factor = carried_block[:, :panel_width]
    projected = carried_block[:, panel_width:]
    basis_local = lower_solve(lower_factor, snapshot_panel)
    return (basis_local * root_rows, lower_factor.T / root_rows, projected / root_rows)


def solution(mesh):
    return jax.shard_map(
        body,
        mesh=mesh,
        in_specs=(P(None, ("gx", "gy")), P(None, ("gx", "gy"))),
        out_specs=(P(None, ("gx", "gy")), P(), P()),
        check_vma=False,
    )
```

profile of v0, /device:TPU:0, one launch (start us, length us, event | category | flops | bytes accessed | tf_op | source)
XLA Modules:
  0.0 134.8 jit_solution(15008608590823437636)
XLA Ops:
  0.6 1.0 copy-done
  2.3 5.8 %cholesky.104 = f32[64,64]{1,0:T(8,128)S(1)} custom-call(f32[64,64]{1,0:T(8,128)S(1)} %fusion.22), custom_call_target="Cholesky" | custom-call | tf_op jit(solution)/shard_map/jit(cholesky)/cholesky | solution.py:51
  8.9 0.7 select_bitcast_fusion.4
  9.5 4.9 %custom-call.15 = f32[1,64,64]{1,2,0:T(8,128)S(1)} custom-call(f32[1,64,64]{2,1,0:T(8,128)S(1)} %get-tuple-element.16), custom_call_target="InvertDiagBlocksLowerTriangular" | custom-call | tf_op jit(solution)/shard_map/jit(_solve_triangular)/triangular_solve | solution.py:34
  14.4 9.7 %fusion.45 = f32[64,960]{1,0:T(8,128)S(1)} fusion(f32[64,2048]{1,0:T(8,128)S(1)} %copy-done, f32[960,2048]{1,0:T(8,128)} %param.6), kind=kOutput, calls=%fused_computation.90 | convolution fusion | flops 1509949440 | bytes 8634368 | tf_op jit(solution)/shard_map/dot_general | solution.py:20
  24.7 3.0 %collective-permute-start = (f32[64,1024]{1,0:T(8,128)S(1)}, f32[64,1024]{1,0:T(8,128)S(1)}, u32[]{:S(2)}, u32[]{:S(2)}) collective-permute-start(f32[64,1024]{1,0:T(8,128)S(1)} %pad_maximum_fusion), channel_id=1, source_target_pairs={{0,4},{4,0},{8,12},{12,8},{16,20},{20,16},{24,28},{28,24},{1,5},{5... | collective-permute-start | bytes 786440 | tf_op jit(solution)/shard_map/ppermute | solution.py:16
  28.3 5.7 %collective-permute-done = f32[64,1024]{1,0:T(8,128)S(1)} collective-permute-done((f32[64,1024]{1,0:T(8,128)S(1)}, f32[64,1024]{1,0:T(8,128)S(1)}, u32[]{:S(2)}, u32[]{:S(2)}) %collective-permute-start) | collective-permute-done | bytes 262176 | tf_op jit(solution)/shard_map/ppermute | solution.py:16
  34.4 5.8 %cholesky.115 = f32[64,64]{1,0:T(8,128)S(1)} custom-call(f32[64,64]{1,0:T(8,128)S(1)} %fusion.19), custom_call_target="Cholesky" | custom-call | tf_op jit(solution)/shard_map/jit(cholesky)/cholesky | solution.py:41
  40.9 0.7 select_bitcast_fusion.3
  41.5 4.9 %custom-call.16 = f32[1,64,64]{1,2,0:T(8,128)S(1)} custom-call(f32[1,64,64]{2,1,0:T(8,128)S(1)} %get-tuple-element.14), custom_call_target="InvertDiagBlocksLowerTriangular" | custom-call | tf_op jit(solution)/shard_map/jit(_solve_triangular)/triangular_solve | solution.py:34
  47.5 1.9 %collective-permute-start.1 = (f32[64,1024]{1,0:T(8,128)S(1)}, f32[64,1024]{1,0:T(8,128)S(1)}, u32[]{:S(2)}, u32[]{:S(2)}) collective-permute-start(f32[64,1024]{1,0:T(8,128)S(1)} %pad_maximum_fusion.1), channel_id=1, source_target_pairs={{0,8},{8,0},{4,12},{12,4},{16,24},{24,16},{20,28},{28,20},{1,9},{9... | collective-permute-start | bytes 786440 | tf_op jit(solution)/shard_map/ppermute | solution.py:16
  49.9 5.1 %collective-permute-done.1 = f32[64,1024]{1,0:T(8,128)S(1)} collective-permute-done((f32[64,1024]{1,0:T(8,128)S(1)}, f32[64,1024]{1,0:T(8,128)S(1)}, u32[]{:S(2)}, u32[]{:S(2)}) %collective-permute-start.1) | collective-permute-done | bytes 262176 | tf_op jit(solution)/shard_map/ppermute | solution.py:16
  55.3 5.8 %cholesky.126 = f32[64,64]{1,0:T(8,128)S(1)} custom-call(f32[64,64]{1,0:T(8,128)S(1)} %fusion.16), custom_call_target="Cholesky" | custom-call | tf_op jit(solution)/shard_map/jit(cholesky)/cholesky | solution.py:41
  61.9 0.7 select_bitcast_fusion.2
  62.5 4.9 %custom-call.17 = f32[1,64,64]{1,2,0:T(8,128)S(1)} custom-call(f32[1,64,64]{2,1,0:T(8,128)S(1)} %get-tuple-element.12), custom_call_target="InvertDiagBlocksLowerTriangular" | custom-call | tf_op jit(solution)/shard_map/jit(_solve_triangular)/triangular_solve | solution.py:34
  68.5 2.6 %collective-permute-start.2 = (f32[64,1024]{1,0:T(8,128)S(1)}, f32[64,1024]{1,0:T(8,128)S(1)}, u32[]{:S(2)}, u32[]{:S(2)}) collective-permute-start(f32[64,1024]{1,0:T(8,128)S(1)} %pad_maximum_fusion.2), channel_id=1, source_target_pairs={{0,16},{16,0},{4,20},{20,4},{8,24},{24,8},{12,28},{28,12},{1,17},{... | collective-permute-start | bytes 786440 | tf_op jit(solution)/shard_map/ppermute | solution.py:16
  71.6 10.0 %collective-permute-done.2 = f32[64,1024]{1,0:T(8,128)S(1)} collective-permute-done((f32[64,1024]{1,0:T(8,128)S(1)}, f32[64,1024]{1,0:T(8,128)S(1)}, u32[]{:S(2)}, u32[]{:S(2)}) %collective-permute-start.2) | collective-permute-done | bytes 262176 | tf_op jit(solution)/shard_map/ppermute | solution.py:16
  81.9 5.8 %cholesky.137 = f32[64,64]{1,0:T(8,128)S(1)} custom-call(f32[64,64]{1,0:T(8,128)S(1)} %fusion.13), custom_call_target="Cholesky" | custom-call | tf_op jit(solution)/shard_map/jit(cholesky)/cholesky | solution.py:41
  88.4 0.7 select_bitcast_fusion.1
  89.1 4.9 %custom-call.18 = f32[1,64,64]{1,2,0:T(8,128)S(1)} custom-call(f32[1,64,64]{2,1,0:T(8,128)S(1)} %get-tuple-element.10), custom_call_target="InvertDiagBlocksLowerTriangular" | custom-call | tf_op jit(solution)/shard_map/jit(_solve_triangular)/triangular_solve | solution.py:34
  95.7 1.0 collective-permute-done.3
  96.9 5.8 %cholesky.148 = f32[64,64]{1,0:T(8,128)S(1)} custom-call(f32[64,64]{1,0:T(8,128)S(1)} %fusion.10), custom_call_target="Cholesky" | custom-call | tf_op jit(solution)/shard_map/jit(cholesky)/cholesky | solution.py:41
  104.1 4.9 %custom-call.19 = f32[1,64,64]{1,2,0:T(8,128)S(1)} custom-call(f32[1,64,64]{2,1,0:T(8,128)S(1)} %get-tuple-element.8), custom_call_target="InvertDiagBlocksLowerTriangular" | custom-call | tf_op jit(solution)/shard_map/jit(_solve_triangular)/triangular_solve | solution.py:34
  109.0 0.7 convolution_add_fusion.1
  110.3 1.1 collective-permute-start.4
  112.0 6.7 %collective-permute-done.4 = f32[64,1024]{1,0:T(8,128)S(1)} collective-permute-done((f32[64,1024]{1,0:T(8,128)S(1)}, f32[64,1024]{1,0:T(8,128)S(1)}, u32[]{:S(2)}, u32[]{:S(2)}) %collective-permute-start.4) | collective-permute-done | bytes 262176 | tf_op jit(solution)/shard_map/ppermute | solution.py:16
  119.0 5.8 %cholesky.159 = f32[64,64]{1,0:T(8,128)S(1)} custom-call(f32[64,64]{1,0:T(8,128)S(1)} %fusion.7), custom_call_target="Cholesky" | custom-call | tf_op jit(solution)/shard_map/jit(cholesky)/cholesky | solution.py:41
  125.5 0.7 multiply_bitcast_fusion
  126.2 0.7 copy.21
  126.9 4.9 %custom-call.9 = f32[1,64,64]{1,2,0:T(8,128)S(1)} custom-call(f32[1,64,64]{2,1,0:T(8,128)S(1)} %get-tuple-element.19), custom_call_target="InvertDiagBlocksLowerTriangular" | custom-call | tf_op jit(solution)/shard_map/jit(_solve_triangular)/triangular_solve | solution.py:34
  131.8 1.4 %convolution_multiply_fusion = f32[64,2048]{1,0:T(8,128)} fusion(f32[64,2048]{1,0:T(8,128)S(1)} %copy-done, f32[1,64,64]{1,2,0:T(8,128)S(1)} %custom-call.9), kind=kOutput, calls=%fused_computation | convolution fusion | flops 100794368 | bytes 1064960 | tf_op jit(solution)/shard_map/jit(_solve_triangular)/triangular_solve | solution.py:34
  133.7 1.1 convolution_multiply_fusion.1
  (57 shorter events, 14.1 us)
Async XLA Ops:
  0.6 1.0 copy-start
  24.7 9.3 %collective-permute-start = (f32[64,1024]{1,0:T(8,128)S(1)}, f32[64,1024]{1,0:T(8,128)S(1)}, u32[]{:S(2)}, u32[]{:S(2)}) collective-permute-start(f32[64,1024]{1,0:T(8,128)S(1)} %pad_maximum_fusion), channel_id=1, source_target_pairs={{0,4},{4,0},{8,12},{12,8},{16,20},{20,16},{24,28},{28,24},{1,5},{5... | collective-permute-start | bytes 786440 | tf_op jit(solution)/shard_map/ppermute | solution.py:16
  47.5 7.6 %collective-permute-start.1 = (f32[64,1024]{1,0:T(8,128)S(1)}, f32[64,1024]{1,0:T(8,128)S(1)}, u32[]{:S(2)}, u32[]{:S(2)}) collective-permute-start(f32[64,1024]{1,0:T(8,128)S(1)} %pad_maximum_fusion.1), channel_id=1, source_target_pairs={{0,8},{8,0},{4,12},{12,4},{16,24},{24,16},{20,28},{28,20},{1,9},{9... | collective-permute-start | bytes 786440 | tf_op jit(solution)/shard_map/ppermute | solution.py:16
  68.5 13.1 %collective-permute-start.2 = (f32[64,1024]{1,0:T(8,128)S(1)}, f32[64,1024]{1,0:T(8,128)S(1)}, u32[]{:S(2)}, u32[]{:S(2)}) collective-permute-start(f32[64,1024]{1,0:T(8,128)S(1)} %pad_maximum_fusion.2), channel_id=1, source_target_pairs={{0,16},{16,0},{4,20},{20,4},{8,24},{24,8},{12,28},{28,12},{1,17},{... | collective-permute-start | bytes 786440 | tf_op jit(solution)/shard_map/ppermute | solution.py:16
  95.0 1.6 %collective-permute-start.3 = (f32[64,1024]{1,0:T(8,128)S(1)}, f32[64,1024]{1,0:T(8,128)S(1)}, u32[]{:S(2)}, u32[]{:S(2)}) collective-permute-start(f32[64,1024]{1,0:T(8,128)S(1)} %pad_maximum_fusion.3), channel_id=1, source_target_pairs={{0,1},{1,0},{2,3},{3,2},{4,5},{5,4},{6,7},{7,6},{8,9},{9,8},{10,11... | collective-permute-start | bytes 786440 | tf_op jit(solution)/shard_map/ppermute | solution.py:16
  110.3 8.4 %collective-permute-start.4 = (f32[64,1024]{1,0:T(8,128)S(1)}, f32[64,1024]{1,0:T(8,128)S(1)}, u32[]{:S(2)}, u32[]{:S(2)}) collective-permute-start(f32[64,1024]{1,0:T(8,128)S(1)} %pad_maximum_fusion.4), channel_id=1, source_target_pairs={{0,2},{2,0},{1,3},{3,1},{4,6},{6,4},{5,7},{7,5},{8,10},{10,8},{9,1... | collective-permute-start | bytes 786440 | tf_op jit(solution)/shard_map/ppermute | solution.py:16
where the time goes:
time: 135 us
  other arithmetic  73.1 us (54%)
  waiting for transfers between devices  28.6 us (21%)
  matrix products  21.2 us (16%)
  starting transfers between devices  8.67 us (6%)
  local copies, waits for them, and re-layouts  2.18 us (2%)
    another operation x11, other arithmetic, lower_solve(): return jax.scipy.linalg.solve_triangular(lower_factor, values, lower=True)  32.6 us
    another operation x15, other arithmetic, merge_blocks(): merged_lower = jnp.linalg.cholesky(summed_gram)  32.6 us
    ppermute x5, waiting for transfers between devices, swapped(): return lax.ppermute(block, axis, route)  28.6 us
    dot_general x12, matrix products, inner_product(): lax.dot_general(left, right, (((1,), (1,)), ((), ())), precision=lax.Prec...  12.2 us
    ppermute x5, starting transfers between devices, swapped(): return lax.ppermute(block, axis, route)  8.67 us
    another operation x3, other arithmetic, body(): jnp.linalg.cholesky(inner_product(snapshot_panel, snapshot_panel))  6.52 us
    another operation x7, matrix products, lower_solve(): return jax.scipy.linalg.solve_triangular(lower_factor, values, lower=True)  4.61 us
    dot_general x10, matrix products, plain_product(): jnp.dot(left, right, precision=lax.Precision.HIGHEST, preferred_element_t...  4.44 us
  transfers between devices with their start and end apart: 5, of which 5 were waited for; matrix products, arithmetic and copies ran while one was open for 2% of the time, Pallas kernels for 0%

commit v1 on v0

v1 whole, which is shorter than its diff:
```python
import math

import jax
import jax.numpy as jnp
from jax import lax
from jax.sharding import PartitionSpec as P


def inner_product(left, right):
    return lax.dot_general(
        left,
        right,
        (((1,), (1,)), ((), ())),
        precision=lax.Precision.HIGHEST,
        preferred_element_type=jnp.float32,
    )


def lower_solve(lower_factor, values):
    return jax.scipy.linalg.solve_triangular(lower_factor, values, lower=True)


def body(snapshot_panel, following):
    panel_width = snapshot_panel.shape[0]
    root_rows = math.sqrt(snapshot_panel.shape[1] * lax.axis_size(("gx", "gy")))
    local = jnp.concatenate(
        [inner_product(snapshot_panel, snapshot_panel), inner_product(snapshot_panel, following)],
        axis=1,
    )
    summed = lax.psum(local, ("gx", "gy"))
    lower_factor = jnp.linalg.cholesky(summed[:, :panel_width])
    projected = lower_solve(lower_factor, summed[:, panel_width:])
    basis_local = lower_solve(lower_factor, snapshot_panel)
    return (basis_local * root_rows, lower_factor.T / root_rows, projected / root_rows)


def solution(mesh):
    return jax.shard_map(
        body,
        mesh=mesh,
        in_specs=(P(None, ("gx", "gy")), P(None, ("gx", "gy"))),
        out_specs=(P(None, ("gx", "gy")), P(), P()),
        check_vma=False,
    )
```

time: 135 us -> 174 us (1.29)
  waiting for transfers between devices: 28.6 us -> 131 us
  other arithmetic: 73.1 us -> 13.7 us
  between operations: 1.02 us -> 14.1 us
  starting transfers between devices: 8.67 us -> 0.04 us
  matrix products: 21.2 us -> 13 us
    psum x0 -> x1, waiting for transfers between devices: none -> 131 us  [body(): summed = lax.psum(local, ('gx', 'gy'))]
    another operation x18 -> x3, other arithmetic: 39.1 us -> 6.52 us  [body(): lower_factor = jnp.linalg.cholesky(summed[:, :panel_width])]
    ppermute x5 -> x0, waiting for transfers between devices: 28.6 us -> none  [swapped(): return lax.ppermute(block, axis, route)]
    another operation x11 -> x1, other arithmetic: 32.6 us -> 4.89 us  [lower_solve(): return jax.scipy.linalg.solve_triangular(lower_factor, values, lower=True)]
    ppermute x5 -> x0, starting transfers between devices: 8.67 us -> none  [swapped(): return lax.ppermute(block, axis, route)]
    dot_general x10 -> x0, matrix products: 4.44 us -> none  [plain_product(): jnp.dot(left, right, precision=lax.Precision.HIGHEST, preferred_element_t...]
    dot_general x12 -> x2, matrix products: 12.2 us -> 9.11 us  [inner_product(): lax.dot_general(left, right, (((1,), (1,)), ((), ())), precision=lax.Prec...]
    another operation x7 -> x2, matrix products: 4.61 us -> 3.87 us  [lower_solve(): return jax.scipy.linalg.solve_triangular(lower_factor, values, lower=True)]
  transfers between devices with their start and end apart: 5 -> 1, of which waited for: 5 -> 1; matrix products, arithmetic and copies ran while one was open for 2% -> 0% of each run, Pallas kernels for 0% -> 0%
where the time goes in v1:
time: 174 us
  waiting for transfers between devices  131 us (75%)
  between operations  14.1 us (8%)
  other arithmetic  13.7 us (8%)
  matrix products  13 us (7%)
  local copies, waits for them, and re-layouts  2.53 us (1%)
    psum x1, waiting for transfers between devices, body(): summed = lax.psum(local, ('gx', 'gy'))  131 us
    dot_general x2, matrix products, inner_product(): lax.dot_general(left, right, (((1,), (1,)), ((), ())), precision=lax.Prec...  9.11 us
    another operation x3, other arithmetic, body(): lower_factor = jnp.linalg.cholesky(summed[:, :panel_width])  6.52 us
    another operation x1, other arithmetic, lower_solve(): return jax.scipy.linalg.solve_triangular(lower_factor, values, lower=True)  4.89 us
    another operation x2, matrix products, lower_solve(): return jax.scipy.linalg.solve_triangular(lower_factor, values, lower=True)  3.87 us
  transfers between devices with their start and end apart: 1, of which 1 were waited for; matrix products, arithmetic and copies ran while one was open for 0% of the time, Pallas kernels for 0%

profile of v1, /device:TPU:0, one launch (start us, length us, event | category | flops | bytes accessed | tf_op | source)
XLA Modules:
  0.0 173.9 jit_solution(6525706086097874623)
XLA Ops:
  7.2 0.0 copy-start
  7.2 0.0 all-reduce.2.cloned.1.call-start
  7.2 1.0 copy-done
  8.2 0.6 fusion.4
  8.8 8.5 %fusion.5 = f32[64,960]{0,1:T(8,128)S(1)} fusion(f32[64,2048]{1,0:T(8,128)S(1)} %copy-done, f32[960,2048]{1,0:T(8,128)} %param.3), kind=kOutput, calls=%fused_computation.16 | convolution fusion | flops 1509949440 | bytes 8634368 | tf_op jit(solution)/shard_map/dot_general | solution.py:10
  17.3 0.8 pad_maximum_fusion
  18.2 0.0 all-reduce.2.cloned.1.call-update
  18.2 130.6 %all-reduce.2.cloned.1.call-done = f32[64,1024]{0,1:T(8,128)} async-done(((f32[64,1024]{0,1:T(8,128)}), f32[64,1024]{0,1:T(8,128)}) %all-reduce.2.cloned.1.call-update) | async-done | bytes 262160 | tf_op jit(solution)/shard_map/psum | solution.py:30
  148.8 0.8 slice.24
  149.6 0.1 copy.7
  149.7 0.8 fusion.3
  150.4 5.8 %cholesky.16 = f32[64,64]{1,0:T(8,128)S(1)} custom-call(f32[64,64]{1,0:T(8,128)S(1)} %fusion.3), custom_call_target="Cholesky" | custom-call | tf_op jit(solution)/shard_map/jit(cholesky)/cholesky | solution.py:31
  156.3 0.6 compare_reduce_fusion
  157.0 0.7 multiply_bitcast_fusion
  157.6 0.7 copy.8
  158.3 4.9 %custom-call.10 = f32[1,64,64]{1,2,0:T(8,128)S(1)} custom-call(f32[1,64,64]{2,1,0:T(8,128)S(1)} %get-tuple-element.7), custom_call_target="InvertDiagBlocksLowerTriangular" | custom-call | tf_op jit(solution)/shard_map/jit(_solve_triangular)/triangular_solve | solution.py:20
  163.2 1.4 convolution_multiply_fusion
  164.7 2.4 %convolution_multiply_fusion.1 = f32[64,960]{1,0:T(8,128)} fusion(f32[64,1024]{0,1:T(8,128)} %all-reduce.2.cloned.1.call-done, f32[1,64,64]{1,2,0:T(8,128)S(1)} %custom-call.10), kind=kOutput, calls=%fused_computation.1 | convolution fusion | flops 47247360 | bytes 753664 | tf_op jit(solution)/shard_map/jit(_solve_triangular)/triangular_solve | solution.py:20
  (1 shorter events, 0.0 us)
Async XLA Ops:
  7.2 1.0 copy-start
  7.2 141.6 %all-reduce.2.cloned.1.call-start = ((), (), s32[]{:S(2)}) async-start(), calls=%async_computation | async-start | bytes 1048576 | tf_op jit(solution)/shard_map/psum | solution.py:30
Sparse Core Ops, SparseCore 0:
  18.3 130.4 all-reduce.1

commit v2 on v1

v2 whole, which is shorter than its diff:
```python
import functools
import math

import jax
import jax.numpy as jnp
from jax import lax
from jax.experimental import pallas as pl
from jax.experimental.pallas import tpu as pltpu
from jax.sharding import PartitionSpec as P

MESH = pl.DeviceIdType.MESH
LANES = 128


def halves(values):
    high = values.astype(jnp.bfloat16)
    return high, (values - high.astype(jnp.float32)).astype(jnp.bfloat16)


def rows_product(left, right):
    return lax.dot_general(
        left, right, (((1,), (1,)), ((), ())), preferred_element_type=jnp.float32
    )


def ordered_sum(own_ref, slots_ref, me, count):
    result = jnp.zeros(own_ref.shape, own_ref.dtype)
    for source in range(count):
        back = lax.rem(me - source + count, count)
        taken = slots_ref[lax.max(back - 1, 0)]
        result = result + jnp.where(back == 0, own_ref[...], taken)
    return result


def sum_kernel(
    n_gx,
    n_gy,
    panel_ref,
    following_ref,
    sums_ref,
    gram_ref,
    panel_vmem,
    rows_vmem,
    panel_split,
    part,
    gram_own,
    gram_gy,
    gram_mid,
    gram_gx,
    half_in,
    half_sum,
    piece_in,
    total,
    load_panel_sem,
    load_sem,
    gy_send,
    gy_recv,
    gx_send,
    gx_recv,
    half_send,
    half_recv,
    rs_send,
    rs_recv,
    ag_send,
    ag_recv,
    back_send,
    back_recv,
):
    width = panel_ref.shape[0]
    units = rows_vmem.shape[0] // width
    blocks = rows_vmem.shape[0] // LANES
    half_blocks = blocks // 2
    half_rows = half_blocks * width
    n_chips = n_gx * n_gy // 2
    piece = half_rows // n_chips
    me_x, me_y = lax.axis_index("gx"), lax.axis_index("gy")
    core = lax.rem(me_y, 2)
    other = 1 - core
    chip = me_x * (n_gy // 2) + me_y // 2
    sibling = (me_x, me_y + 1 - 2 * core)

    def chip_device(index):
        return (index // (n_gy // 2), lax.rem(index, n_gy // 2) * 2 + core)

    load_panel = pltpu.make_async_copy(panel_ref, panel_vmem, load_panel_sem)
    load_panel.start()

    def load(source, unit):
        pltpu.make_async_copy(
            source, rows_vmem.at[pl.ds(unit * width, width)], load_sem.at[unit]
        ).start()

    for step in range(units):
        unit = lax.rem(step + other * (units // 2), units)
        if step % (units // 2) != units // 2 - 1:
            load(following_ref.at[pl.ds(unit * width, width)], unit)
        else:
            @pl.when(unit == units - 1)
            def _():
                load(panel_ref, unit)

            @pl.when(unit != units - 1)
            def _():
                load(following_ref.at[pl.ds(unit * width, width)], unit)

    barrier = pltpu.get_barrier_semaphore()
    n_signals = 0
    for k in range(1, n_chips):
        pl.semaphore_signal(
            barrier, inc=1, device_id=chip_device(lax.rem(chip + k, n_chips)), device_id_type=MESH
        )
        n_signals += 1
    for k in range(1, n_gy, 2):
        pl.semaphore_signal(
            barrier, inc=1, device_id=(me_x, lax.rem(me_y + k, n_gy)), device_id_type=MESH
        )
        n_signals += 1

    load_panel.wait()
    high, low = halves(panel_vmem[...])
    panel_split[0:width, :] = high
    panel_split[width : 2 * width, :] = low
    quads = rows_product(panel_split[...], panel_split[...])
    pair = quads[:width] + quads[width:]
    gram = pair[:, :width] + pair[:, width:]
    gram_own[...] = jnp.concatenate([gram[: width // 2], gram[width // 2 :]], axis=1)

    pl.semaphore_wait(barrier, n_signals)

    gy_copies = []
    for k in range(1, n_gy):
        copy = pltpu.make_async_remote_copy(
            src_ref=gram_own,
            dst_ref=gram_gy.at[k - 1],
            send_sem=gy_send.at[k - 1],
            recv_sem=gy_recv.at[k - 1],
            device_id=(me_x, lax.rem(me_y + k, n_gy)),
            device_id_type=MESH,
        )
        copy.start()
        gy_copies.append(copy)

    def cross(block):
        for unit in (2 * block, 2 * block + 1):
            pltpu.make_async_copy(
                panel_ref, rows_vmem.at[pl.ds(unit * width, width)], load_sem.at[unit]
            ).wait()
        row_high, row_low = halves(rows_vmem[pl.ds(block * LANES, LANES), :])
        split = panel_split[...]
        turned = (rows_product(row_high, split) + rows_product(row_low, split)).T
        part[pl.ds(block * width, width), :] = turned[:width] + turned[width:]

    @pl.loop(0, half_blocks)
    def _(i):
        cross(other * half_blocks + i)

    half_copy = pltpu.make_async_remote_copy(
        src_ref=part.at[pl.ds(other * half_rows, half_rows)],
        dst_ref=half_in,
        send_sem=half_send,
        recv_sem=half_recv,
        device_id=sibling,
        device_id_type=MESH,
    )
    half_copy.start()

    for copy in gy_copies:
        copy.wait_recv()
    gram_mid[...] = ordered_sum(gram_own, gram_gy, me_y, n_gy)
    gx_copies = []
    for k in range(1, n_gx):
        copy = pltpu.make_async_remote_copy(
            src_ref=gram_mid,
            dst_ref=gram_gx.at[k - 1],
            send_sem=gx_send.at[k - 1],
            recv_sem=gx_recv.at[k - 1],
            device_id=(lax.rem(me_x + k, n_gx), me_y),
            device_id_type=MESH,
        )
        copy.start()
        gx_copies.append(copy)

    @pl.loop(0, half_blocks)
    def _(i):
        cross(core * half_blocks + i)

    half_copy.wait_recv()
    half_sum[...] = part[pl.ds(core * half_rows, half_rows), :] + half_in[...]
    rs_copies = []
    for k in range(1, n_chips):
        to = lax.rem(chip + k, n_chips)
        copy = pltpu.make_async_remote_copy(
            src_ref=half_sum.at[pl.ds(to * piece, piece)],
            dst_ref=piece_in.at[k - 1],
            send_sem=rs_send.at[k - 1],
            recv_sem=rs_recv.at[k - 1],
            device_id=chip_device(to),
            device_id_type=MESH,
        )
        copy.start()
        rs_copies.append(copy)

    for copy in gx_copies:
        copy.wait_recv()
    gram_ref[...] = ordered_sum(gram_mid, gram_gx, me_x, n_gx)

    for copy in rs_copies:
        copy.wait_recv()
    own_start = core * half_rows + chip * piece
    own = half_sum[pl.ds(chip * piece, piece), :]
    for k in range(n_chips - 1):
        own = own + piece_in[k]
    total[pl.ds(own_start, piece), :] = own

    ag_copies = []
    for k in range(1, n_chips):
        copy = pltpu.make_async_remote_copy(
            src_ref=total.at[pl.ds(own_start, piece)],
            dst_ref=total.at[pl.ds(own_start, piece)],
            send_sem=ag_send.at[k - 1],
            recv_sem=ag_recv.at[k - 1],
            device_id=chip_device(lax.rem(chip + k, n_chips)),
            device_id_type=MESH,
        )
        copy.start()
        ag_copies.append(copy)
    for copy in ag_copies:
        copy.wait_recv()
    back_copy = pltpu.make_async_remote_copy(
        src_ref=total.at[pl.ds(core * half_rows, half_rows)],
        dst_ref=total.at[pl.ds(core * half_rows, half_rows)],
        send_sem=back_send,
        recv_sem=back_recv,
        device_id=sibling,
        device_id_type=MESH,
    )
    back_copy.start()
    back_copy.wait_recv()
    sums_ref[...] = total[...]
    back_copy.wait_send()
    for copy in gy_copies + gx_copies + [half_copy] + rs_copies + ag_copies:
        copy.wait_send()


def summed_blocks(panel, following, n_gx, n_gy):
    width, cells = panel.shape
    rows = width + following.shape[0]
    all_rows = rows // LANES * width
    half_rows = all_rows // 2
    n_chips = n_gx * n_gy // 2
    piece = half_rows // n_chips
    gram_block = (width // 2, 2 * width)
    dma = pltpu.SemaphoreType.DMA
    f32 = jnp.float32
    return pl.pallas_call(
        functools.partial(sum_kernel, n_gx, n_gy),
        out_shape=(
            jax.ShapeDtypeStruct((all_rows, LANES), f32),
            jax.ShapeDtypeStruct(gram_block, f32),
        ),
        in_specs=[pl.BlockSpec(memory_space=pl.ANY)] * 2,
        out_specs=(pl.BlockSpec(memory_space=pltpu.VMEM),) * 2,
        scratch_shapes=[
            pltpu.VMEM((width, cells), f32),
            pltpu.VMEM((rows, cells), f32),
            pltpu.VMEM((2 * width, cells), jnp.bfloat16),
            pltpu.VMEM((all_rows, LANES), f32),
            pltpu.VMEM(gram_block, f32),
            pltpu.VMEM((n_gy - 1,) + gram_block, f32),
            pltpu.VMEM(gram_block, f32),
            pltpu.VMEM((n_gx - 1,) + gram_block, f32),
            pltpu.VMEM((half_rows, LANES), f32),
            pltpu.VMEM((half_rows, LANES), f32),
            pltpu.VMEM((n_chips - 1, piece, LANES), f32),
            pltpu.VMEM((all_rows, LANES), f32),
            dma,
            dma((rows // width,)),
            dma((n_gy - 1,)),
            dma((n_gy - 1,)),
            dma((n_gx - 1,)),
            dma((n_gx - 1,)),
            dma,
            dma,
            dma((n_chips - 1,)),
            dma((n_chips - 1,)),
            dma((n_chips - 1,)),
            dma((n_chips - 1,)),
            dma,
            dma,
        ],
        compiler_params=pltpu.CompilerParams(
            collective_id=0, has_side_effects=True, vmem_limit_bytes=40 * 2**20
        ),
        name="sum_blocks",
    )(panel, following)


def eliminate(gram, out_ref):
    width = gram.shape[0]
    row = lax.broadcasted_iota(jnp.int32, (width, width), 0)
    column = lax.broadcasted_iota(jnp.int32, (width, width), 1)
    wide = jnp.concatenate([gram, jnp.where(row == column, 1.0, 0.0)], axis=1)
    n_groups = width // 8
    sublane = lax.broadcasted_iota(jnp.int32, (8, 2 * width), 0)
    group = [wide[8 * g : 8 * g + 8, :] for g in range(n_groups)]
    step = 4
    for first in range(0, width, step):
        g0 = first // 8
        live = range(g0, n_groups)
        columns = [
            {
                g: jnp.broadcast_to(group[g][:, first + k : first + k + 1], (8, 2 * width))
                for g in live
            }
            for k in range(step)
        ]
        for k in range(step):
            r = (first + k) % 8
            pivot_row = group[g0][r : r + 1, :]
            pivot = columns[k][g0][r : r + 1, :]
            inverse = 1.0 / pivot
            out_ref[first + k : first + k + 1, :] = pivot_row * lax.rsqrt(pivot)
            scaled_row = pivot_row * inverse
            heads = [columns[l][g0][r : r + 1, :] * inverse for l in range(k + 1, step)]
            for g in live:
                factor = columns[k][g]
                if g == g0:
                    factor = jnp.where(sublane > r, factor, 0.0)
                group[g] = group[g] - factor * scaled_row
                for l in range(k + 1, step):
                    columns[l][g] = columns[l][g] - factor * heads[l - k - 1]


def factor_kernel(root_rows, sums_ref, gram_ref, panel_ref, basis_ref, upper_ref, proj_ref, wide_ref):
    width, cells = panel_ref.shape
    packed = gram_ref[...]
    eliminate(jnp.concatenate([packed[:, :width], packed[:, width:]], axis=0), wide_ref)
    row = lax.broadcasted_iota(jnp.int32, (width, width), 0)
    column = lax.broadcasted_iota(jnp.int32, (width, width), 1)
    wide = wide_ref[...]
    upper_ref[...] = jnp.where(column >= row, wide[:, :width], 0.0) * (1.0 / root_rows)
    high, low = halves(wide[:, width:])
    stacked = jnp.concatenate([high, high, low, low], axis=1)

    def apply(values):
        value_high, value_low = halves(values)
        return jnp.dot(
            stacked,
            jnp.concatenate([value_high, value_low, value_high, value_low], axis=0),
            preferred_element_type=jnp.float32,
        )

    for start in range(0, proj_ref.shape[1], LANES):
        count = min(LANES, proj_ref.shape[1] - start)
        first = start // LANES * width
        proj_ref[:, start : start + count] = (
            apply(sums_ref[first : first + width, :]) * (1.0 / root_rows)
        )[:, :count]
    chunk = 256
    for start in range(0, cells, chunk):
        basis_ref[:, start : start + chunk] = (
            apply(panel_ref[:, start : start + chunk]) * root_rows
        )


def factored(sums, gram, panel, next_count, root_rows):
    width, cells = panel.shape
    f32 = jnp.float32
    return pl.pallas_call(
        functools.partial(factor_kernel, root_rows),
        out_shape=(
            jax.ShapeDtypeStruct((width, cells), f32),
            jax.ShapeDtypeStruct((width, width), f32),
            jax.ShapeDtypeStruct((width, next_count), f32),
        ),
        scratch_shapes=[pltpu.VMEM((width, 2 * width), f32)],
        compiler_params=pltpu.CompilerParams(vmem_limit_bytes=16 * 2**20),
        name="factor_and_apply",
    )(sums, gram, panel)


def plain_sums(panel, following):
    precise = functools.partial(
        lax.dot_general,
        dimension_numbers=(((1,), (1,)), ((), ())),
        precision=lax.Precision.HIGHEST,
        preferred_element_type=jnp.float32,
    )
    width = panel.shape[0]
    cross = lax.psum(
        jnp.concatenate([precise(panel, following), precise(panel, panel)], axis=1), ("gx", "gy")
    )
    blocks = cross.shape[1] // LANES
    sums = cross.reshape(width, blocks, LANES).transpose(1, 0, 2).reshape(blocks * width, LANES)
    gram = cross[:, -width:]
    return sums, jnp.concatenate([gram[: width // 2], gram[width // 2 :]], axis=1)


def body(n_gx, n_gy, panel, following):
    width, cells = panel.shape
    root_rows = math.sqrt(cells * n_gx * n_gy)
    half_rows = (width + following.shape[0]) // LANES * width // 2
    if half_rows % (8 * (n_gx * n_gy // 2)) == 0:
        sums, gram = summed_blocks(panel, following, n_gx, n_gy)
    else:
        sums, gram = plain_sums(panel, following)
    return factored(sums, gram, panel, following.shape[0], root_rows)


def solution(mesh):
    return jax.shard_map(
        functools.partial(body, mesh.shape["gx"], mesh.shape["gy"]),
        mesh=mesh,
        in_specs=(P(None, ("gx", "gy")), P(None, ("gx", "gy"))),
        out_specs=(P(None, ("gx", "gy")), P(), P()),
        check_vma=False,
    )
```

time: 174 us -> 33.8 us (0.19)
  waiting for transfers between devices: 131 us -> 0 us
  Pallas kernels: 0 us -> 28.7 us
  other arithmetic: 13.7 us -> 0 us
  between operations: 14.1 us -> 0.65 us
  matrix products: 13 us -> 0 us
    psum x1 -> x0, waiting for transfers between devices: 131 us -> none  [body(): summed = lax.psum(local, ('gx', 'gy'))]
    pallas_call x0 -> x2, Pallas kernels: none -> 28.7 us  [the longest x1 25.3 us: summed_blocks(): pl.pallas_call(functools.partial(sum_kernel, n_gx, n_gy), out_shape=(jax....]
    another operation x4 -> x0, other arithmetic: 11.4 us -> none  [the longest x3 6.52 us: body(): lower_factor = jnp.linalg.cholesky(summed[:, :panel_width])]
    dot_general x2 -> x0, matrix products: 9.11 us -> none  [inner_product(): lax.dot_general(left, right, (((1,), (1,)), ((), ())), precision=lax.Prec...]
    another operation x2 -> x0, matrix products: 3.87 us -> none  [lower_solve(): return jax.scipy.linalg.solve_triangular(lower_factor, values, lower=True)]
    unnamed x3 -> x4, local copies, waits for them, and re-layouts: 1.69 us -> 4.27 us
  transfers between devices with their start and end apart: 1 -> 0, of which waited for: 1 -> 0; matrix products, arithmetic and copies ran while one was open for 0% -> 0% of each run, Pallas kernels for 0% -> 0%
where the time goes in v2:
time: 33.8 us; the launch traced here: 33.6 us
  Pallas kernels  28.7 us (85%)
  local copies, waits for them, and re-layouts  4.27 us (13%)
  between operations  0.65 us (2%)
    pallas_call x1, Pallas kernels, summed_blocks(): pl.pallas_call(functools.partial(sum_kernel, n_gx, n_gy), out_shape=(jax....  25.3 us
    unnamed x4, local copies, waits for them, and re-layouts  4.27 us
    pallas_call x1, Pallas kernels, factored(): pl.pallas_call(functools.partial(factor_kernel, root_rows), out_shape=(ja...  3.44 us

profile of v2, /device:TPU:0, one launch (start us, length us, event | category | flops | bytes accessed | tf_op | source)
XLA Modules:
  0.0 33.6 jit_solution(5959514329281526011)
XLA Ops:
  0.6 0.0 copy-start
  0.6 3.2 %copy-done = f32[960,2048]{1,0:T(8,128)S(1)} copy-done((f32[960,2048]{1,0:T(8,128)S(1)}, f32[960,2048]{1,0:T(8,128)}, u32[]{:S(2)}) %copy-start) | copy-done | bytes 7864344
  3.9 0.0 copy-start.1
  3.9 1.0 %copy-done.1 = f32[64,2048]{1,0:T(8,128)S(1)} copy-done((f32[64,2048]{1,0:T(8,128)S(1)}, f32[64,2048]{1,0:T(8,128)}, u32[]{:S(2)}) %copy-start.1) | copy-done | bytes 524312
  4.9 25.3 %sum_blocks.1 = (f32[512,128]{1,0:T(8,128)S(1)}, f32[32,128]{1,0:T(8,128)S(1)}) custom-call(f32[64,2048]{1,0:T(8,128)S(1)} %copy-done.1, f32[960,2048]{1,0:T(8,128)S(1)} %copy-done), custom_call_target="tpu_custom_call" | custom-call | tf_op jit(solution)/shard_map/sum_blocks/pallas_call | solution.py:255
  30.2 3.4 %factor_and_apply.1 = (f32[64,2048]{1,0:T(8,128)}, f32[64,64]{1,0:T(8,128)}, f32[64,960]{1,0:T(8,128)}) custom-call(f32[512,128]{1,0:T(8,128)S(1)} %get-tuple-element.5.sums_ref, f32[32,128]{1,0:T(8,128)S(1)} %get-tuple-element.6.gram_ref, f32[64,2048]{1,0:T(8,128)S(1)} %copy-done.1), custom_call_target="tpu_custom_call" | custom-call | tf_op jit(solution)/shard_map/factor_and_apply/pallas_call | solution.py:369
Async XLA Ops:
  0.6 3.2 %copy-start = (f32[960,2048]{1,0:T(8,128)S(1)}, f32[960,2048]{1,0:T(8,128)}, u32[]{:S(2)}) copy-start(f32[960,2048]{1,0:T(8,128)} %following_ref.1) | copy-start | bytes 23592964
  3.9 1.0 %copy-start.1 = (f32[64,2048]{1,0:T(8,128)S(1)}, f32[64,2048]{1,0:T(8,128)}, u32[]{:S(2)}) copy-start(f32[64,2048]{1,0:T(8,128)} %panel_ref.3) | copy-start | bytes 1572868

commit v3 on v2

--- a/solution.py
+++ b/solution.py
@@ -21,6 +21,42 @@
     return lax.dot_general(
         left, right, (((1,), (1,)), ((), ())), preferred_element_type=jnp.float32
     )
+
+
+def eliminate(gram, out_ref):
+    width = gram.shape[0]
+    row = lax.broadcasted_iota(jnp.int32, (width, width), 0)
+    column = lax.broadcasted_iota(jnp.int32, (width, width), 1)
+    wide = jnp.concatenate([gram, jnp.where(row == column, 1.0, 0.0)], axis=1)
+    n_groups = width // 8
+    sublane = lax.broadcasted_iota(jnp.int32, (8, 2 * width), 0)
+    group = [wide[8 * g : 8 * g + 8, :] for g in range(n_groups)]
+    step = 4
+    for first in range(0, width, step):
+        g0 = first // 8
+        live = range(g0, n_groups)
+        columns = [
+            {
+                g: jnp.broadcast_to(group[g][:, first + k : first + k + 1], (8, 2 * width))
+                for g in live
+            }
+            for k in range(step)
+        ]
+        for k in range(step):
+            r = (first + k) % 8
+            pivot_row = group[g0][r : r + 1, :]
+            pivot = columns[k][g0][r : r + 1, :]
+            inverse = 1.0 / pivot
+            out_ref[first + k : first + k + 1, :] = pivot_row * lax.rsqrt(pivot)
+            scaled_row = pivot_row * inverse
+            heads = [columns[l][g0][r : r + 1, :] * inverse for l in range(k + 1, step)]
+            for g in live:
+                factor = columns[k][g]
+                if g == g0:
+                    factor = jnp.where(sublane > r, factor, 0.0)
+                group[g] = group[g] - factor * scaled_row
+                for l in range(k + 1, step):
+                    columns[l][g] = columns[l][g] - factor * heads[l - k - 1]
 
 
 def ordered_sum(own_ref, slots_ref, me, count):
@@ -38,7 +74,7 @@
     panel_ref,
     following_ref,
     sums_ref,
-    gram_ref,
+    wide_ref,
     panel_vmem,
     rows_vmem,
     panel_split,
@@ -140,19 +176,26 @@
         copy.start()
         gy_copies.append(copy)
 
-    def cross(block):
-        for unit in (2 * block, 2 * block + 1):
+    batch = 2 * LANES
+    half_batches = half_blocks // 2
+
+    def cross(index):
+        for k in range(batch // width):
+            unit = index * (batch // width) + k
             pltpu.make_async_copy(
                 panel_ref, rows_vmem.at[pl.ds(unit * width, width)], load_sem.at[unit]
             ).wait()
-        row_high, row_low = halves(rows_vmem[pl.ds(block * LANES, LANES), :])
-        split = panel_split[...]
-        turned = (rows_product(row_high, split) + rows_product(row_low, split)).T
-        part[pl.ds(block * width, width), :] = turned[:width] + turned[width:]
-
-    @pl.loop(0, half_blocks)
+        row_high, row_low = halves(rows_vmem[pl.ds(index * batch, batch), :])
+        quads = rows_product(jnp.concatenate([row_high, row_low], axis=0), panel_split[...])
+        pair = quads[:batch] + quads[batch:]
+        for k in range(batch // LANES):
+            turned = pair[k * LANES : (k + 1) * LANES].T
+            block = index * (batch // LANES) + k
+            part[pl.ds(block * width, width), :] = turned[:width] + turned[width:]
+
+    @pl.loop(0, half_batches)
     def _(i):
-        cross(other * half_blocks + i)
+        cross(other * half_batches + i)
 
     half_copy = pltpu.make_async_remote_copy(
         src_ref=part.at[pl.ds(other * half_rows, half_rows)],
@@ -180,9 +223,9 @@
         copy.start()
         gx_copies.append(copy)
 
-    @pl.loop(0, half_blocks)
+    @pl.loop(0, half_batches)
     def _(i):
-        cross(core * half_blocks + i)
+        cross(core * half_batches + i)
 
     half_copy.wait_recv()
     half_sum[...] = part[pl.ds(core * half_rows, half_rows), :] + half_in[...]
@@ -202,7 +245,8 @@
 
     for copy in gx_copies:
         copy.wait_recv()
-    gram_ref[...] = ordered_sum(gram_mid, gram_gx, me_x, n_gx)
+    packed = ordered_sum(gram_mid, gram_gx, me_x, n_gx)
+    eliminate(jnp.concatenate([packed[:, :width], packed[:, width:]], axis=0), wide_ref)
 
     for copy in rs_copies:
         copy.wait_recv()
@@ -256,9 +300,9 @@
         functools.partial(sum_kernel, n_gx, n_gy),
         out_shape=(
             jax.ShapeDtypeStruct((all_rows, LANES), f32),
-            jax.ShapeDtypeStruct(gram_block, f32),
+            jax.ShapeDtypeStruct((width, 2 * width), f32),
         ),
-        in_specs=[pl.BlockSpec(memory_space=pl.ANY)] * 2,
+        in_specs=[pl.BlockSpec(memory_space=pltpu.HBM)] * 2,
         out_specs=(pl.BlockSpec(memory_space=pltpu.VMEM),) * 2,
         scratch_shapes=[
             pltpu.VMEM((width, cells), f32),
@@ -289,52 +333,14 @@
             dma,
         ],
         compiler_params=pltpu.CompilerParams(
-            collective_id=0, has_side_effects=True, vmem_limit_bytes=40 * 2**20
+            collective_id=0, has_side_effects=True, vmem_limit_bytes=56 * 2**20
         ),
         name="sum_blocks",
     )(panel, following)
 
 
-def eliminate(gram, out_ref):
-    width = gram.shape[0]
-    row = lax.broadcasted_iota(jnp.int32, (width, width), 0)
-    column = lax.broadcasted_iota(jnp.int32, (width, width), 1)
-    wide = jnp.concatenate([gram, jnp.where(row == column, 1.0, 0.0)], axis=1)
-    n_groups = width // 8
-    sublane = lax.broadcasted_iota(jnp.int32, (8, 2 * width), 0)
-    group = [wide[8 * g : 8 * g + 8, :] for g in range(n_groups)]
-    step = 4
-    for first in range(0, width, step):
-        g0 = first // 8
-        live = range(g0, n_groups)
-        columns = [
-            {
-                g: jnp.broadcast_to(group[g][:, first + k : first + k + 1], (8, 2 * width))
-                for g in live
-            }
-            for k in range(step)
-        ]
-        for k in range(step):
-            r = (first + k) % 8
-            pivot_row = group[g0][r : r + 1, :]
-            pivot = columns[k][g0][r : r + 1, :]
-            inverse = 1.0 / pivot
-            out_ref[first + k : first + k + 1, :] = pivot_row * lax.rsqrt(pivot)
-            scaled_row = pivot_row * inverse
-            heads = [columns[l][g0][r : r + 1, :] * inverse for l in range(k + 1, step)]
-            for g in live:
-                factor = columns[k][g]
-                if g == g0:
-                    factor = jnp.where(sublane > r, factor, 0.0)
-                group[g] = group[g] - factor * scaled_row
-                for l in range(k + 1, step):
-                    columns[l][g] = columns[l][g] - factor * heads[l - k - 1]
-
-
-def factor_kernel(root_rows, sums_ref, gram_ref, panel_ref, basis_ref, upper_ref, proj_ref, wide_ref):
+def apply_kernel(root_rows, sums_ref, wide_ref, panel_ref, basis_ref, upper_ref, proj_ref):
     width, cells = panel_ref.shape
-    packed = gram_ref[...]
-    eliminate(jnp.concatenate([packed[:, :width], packed[:, width:]], axis=0), wide_ref)
     row = lax.broadcasted_iota(jnp.int32, (width, width), 0)
     column = lax.broadcasted_iota(jnp.int32, (width, width), 1)
     wide = wide_ref[...]
@@ -363,20 +369,19 @@
         )
 
 
-def factored(sums, gram, panel, next_count, root_rows):
+def applied(sums, wide, panel, next_count, root_rows):
     width, cells = panel.shape
     f32 = jnp.float32
     return pl.pallas_call(
-        functools.partial(factor_kernel, root_rows),
+        functools.partial(apply_kernel, root_rows),
         out_shape=(
             jax.ShapeDtypeStruct((width, cells), f32),
             jax.ShapeDtypeStruct((width, width), f32),
             jax.ShapeDtypeStruct((width, next_count), f32),
         ),
-        scratch_shapes=[pltpu.VMEM((width, 2 * width), f32)],
-        compiler_params=pltpu.CompilerParams(vmem_limit_bytes=16 * 2**20),
-        name="factor_and_apply",
-    )(sums, gram, panel)
+        compiler_params=pltpu.CompilerParams(vmem_limit_bytes=60 * 2**20),
+        name="apply_factor",
+    )(sums, wide, panel)
 
 
 def plain_sums(panel, following):
@@ -392,8 +397,12 @@
     )
     blocks = cross.shape[1] // LANES
     sums = cross.reshape(width, blocks, LANES).transpose(1, 0, 2).reshape(blocks * width, LANES)
-    gram = cross[:, -width:]
-    return sums, jnp.concatenate([gram[: width // 2], gram[width // 2 :]], axis=1)
+    wide = pl.pallas_call(
+        lambda gram_ref, wide_ref: eliminate(gram_ref[...], wide_ref),
+        out_shape=jax.ShapeDtypeStruct((width, 2 * width), jnp.float32),
+        name="factor",
+    )(cross[:, -width:])
+    return sums, wide
 
 
 def body(n_gx, n_gy, panel, following):
@@ -401,10 +410,10 @@
     root_rows = math.sqrt(cells * n_gx * n_gy)
     half_rows = (width + following.shape[0]) // LANES * width // 2
     if half_rows % (8 * (n_gx * n_gy // 2)) == 0:
-        sums, gram = summed_blocks(panel, following, n_gx, n_gy)
+        sums, wide = summed_blocks(panel, following, n_gx, n_gy)
     else:
-        sums, gram = plain_sums(panel, following)
-    return factored(sums, gram, panel, following.shape[0], root_rows)
+        sums, wide = plain_sums(panel, following)
+    return applied(sums, wide, panel, following.shape[0], root_rows)
 
 
 def solution(mesh):

time: 33.8 us -> 28.6 us (0.85)
  local copies, waits for them, and re-layouts: 4.27 us -> 0 us
  Pallas kernels: 28.7 us -> 27.9 us
    unnamed x4 -> x0, local copies, waits for them, and re-layouts: 4.27 us -> none
    pallas_call x1, Pallas kernels: 3.44 us -> 2.4 us  [applied(): pl.pallas_call(functools.partial(apply_kernel, root_rows), out_shape=(jax...]
where the time goes in v3:
time: 28.6 us; the launch traced here: 28.5 us
  Pallas kernels  27.9 us (98%)
  between operations  0.64 us (2%)
    pallas_call x1, Pallas kernels, summed_blocks(): pl.pallas_call(functools.partial(sum_kernel, n_gx, n_gy), out_shape=(jax....  25.5 us
    pallas_call x1, Pallas kernels, applied(): pl.pallas_call(functools.partial(apply_kernel, root_rows), out_shape=(jax...  2.4 us

profile of v3, /device:TPU:0, one launch (start us, length us, event | category | flops | bytes accessed | tf_op | source)
XLA Modules:
  0.0 28.5 jit_solution(985410645822760808)
XLA Ops:
  0.6 25.5 %sum_blocks.1 = (f32[512,128]{1,0:T(8,128)}, f32[64,128]{1,0:T(8,128)}) custom-call(f32[64,2048]{1,0:T(8,128)} %panel_ref.3, f32[960,2048]{1,0:T(8,128)} %following_ref.1), custom_call_target="tpu_custom_call" | custom-call | tf_op jit(solution)/shard_map/sum_blocks/pallas_call | solution.py:299
  26.1 2.4 %apply_factor.1 = (f32[64,2048]{1,0:T(8,128)}, f32[64,64]{1,0:T(8,128)}, f32[64,960]{1,0:T(8,128)}) custom-call(f32[512,128]{1,0:T(8,128)} %get-tuple-element.5.sums_ref, f32[64,128]{1,0:T(8,128)} %get-tuple-element.6.wide_ref, f32[64,2048]{1,0:T(8,128)} %panel_ref.3), custom_call_target="tpu_custom_call" | custom-call | tf_op jit(solution)/shard_map/apply_factor/pallas_call | solution.py:375

commit v4 on v3

v4 whole, which is shorter than its diff:
```python
import functools
import math

import jax
import jax.numpy as jnp
from jax import lax
from jax.experimental import pallas as pl
from jax.experimental.pallas import tpu as pltpu
from jax.sharding import PartitionSpec as P

MESH = pl.DeviceIdType.MESH
LANES = 128
BATCH = 256


def halves(values):
    high = values.astype(jnp.bfloat16)
    return high, (values - high.astype(jnp.float32)).astype(jnp.bfloat16)


def rows_product(left, right):
    return lax.dot_general(
        left, right, (((1,), (1,)), ((), ())), preferred_element_type=jnp.float32
    )


def eliminate(gram, out_ref):
    width = gram.shape[0]
    row = lax.broadcasted_iota(jnp.int32, (width, width), 0)
    column = lax.broadcasted_iota(jnp.int32, (width, width), 1)
    wide = jnp.concatenate([gram, jnp.where(row == column, 1.0, 0.0)], axis=1)
    n_groups = width // 8
    sublane = lax.broadcasted_iota(jnp.int32, (8, 2 * width), 0)
    group = [wide[8 * g : 8 * g + 8, :] for g in range(n_groups)]
    step = 4
    for first in range(0, width, step):
        g0 = first // 8
        live = range(g0, n_groups)
        columns = [
            {
                g: jnp.broadcast_to(group[g][:, first + k : first + k + 1], (8, 2 * width))
                for g in live
            }
            for k in range(step)
        ]
        for k in range(step):
            r = (first + k) % 8
            pivot_row = group[g0][r : r + 1, :]
            pivot = columns[k][g0][r : r + 1, :]
            inverse = 1.0 / pivot
            out_ref[first + k : first + k + 1, :] = pivot_row * lax.rsqrt(pivot)
            scaled_row = pivot_row * inverse
            heads = [columns[l][g0][r : r + 1, :] * inverse for l in range(k + 1, step)]
            for g in live:
                factor = columns[k][g]
                if g == g0:
                    factor = jnp.where(sublane > r, factor, 0.0)
                group[g] = group[g] - factor * scaled_row
                for l in range(k + 1, step):
                    columns[l][g] = columns[l][g] - factor * heads[l - k - 1]


def write_upper(root_rows, wide_ref, upper_ref):
    width = upper_ref.shape[0]
    row = lax.broadcasted_iota(jnp.int32, (width, width), 0)
    column = lax.broadcasted_iota(jnp.int32, (width, width), 1)
    wide = wide_ref[...]
    upper_ref[...] = jnp.where(column >= row, wide[:, :width], 0.0) * (1.0 / root_rows)
    high, low = halves(wide[:, width:])
    return jnp.concatenate([high, high, low, low], axis=1)


def applied_inverse(stacked, values):
    high, low = halves(values)
    return jnp.dot(
        stacked,
        jnp.concatenate([high, low, high, low], axis=0),
        preferred_element_type=jnp.float32,
    )


def write_projection(root_rows, stacked, sums_ref, proj_ref, block):
    width = stacked.shape[0]
    start = block * LANES
    count = min(LANES, proj_ref.shape[1] - start)
    result = applied_inverse(stacked, sums_ref[block * width : (block + 1) * width, :])
    proj_ref[:, start : start + count] = (result * (1.0 / root_rows))[:, :count]


def write_basis(root_rows, stacked, panel_ref, basis_ref):
    for start in range(0, panel_ref.shape[1], BATCH):
        basis_ref[:, start : start + BATCH] = (
            applied_inverse(stacked, panel_ref[:, start : start + BATCH]) * root_rows
        )


def ordered_sum(own_ref, slots_ref, me, count):
    result = jnp.zeros(own_ref.shape, own_ref.dtype)
    for source in range(count):
        back = lax.rem(me - source + count, count)
        taken = slots_ref[lax.max(back - 1, 0)]
        result = result + jnp.where(back == 0, own_ref[...], taken)
    return result


def sum_kernel(
    n_gx,
    n_gy,
    root_rows,
    panel_ref,
    following_ref,
    basis_ref,
    upper_ref,
    proj_ref,
    wide_ref,
    basis_vmem,
    panel_vmem,
    rows_vmem,
    panel_split,
    part,
    gram_own,
    gram_gy,
    gram_mid,
    gram_gx,
    half_in,
    half_sum,
    piece_in,
    total,
    load_panel_sem,
    store_sem,
    load_sem,
    gy_send,
    gy_recv,
    gx_send,
    gx_recv,
    half_send,
    half_recv,
    rs_send,
    rs_recv,
    ag_send,
    ag_recv,
    back_send,
    back_recv,
):
    width = panel_ref.shape[0]
    units = rows_vmem.shape[0] // width
    half_rows = rows_vmem.shape[0] // LANES * width // 2
    group_rows = BATCH // LANES * width
    n_groups = half_rows // group_rows
    n_chips = n_gx * n_gy // 2
    piece = group_rows // n_chips
    me_x, me_y = lax.axis_index("gx"), lax.axis_index("gy")
    core = lax.rem(me_y, 2)
    other = 1 - core
    chip = me_x * (n_gy // 2) + me_y // 2
    sibling = (me_x, me_y + 1 - 2 * core)

    def chip_device(index):
        return (index // (n_gy // 2), lax.rem(index, n_gy // 2) * 2 + core)

    load_panel = pltpu.make_async_copy(panel_ref, panel_vmem, load_panel_sem)
    load_panel.start()

    def load(source, unit):
        pltpu.make_async_copy(
            source, rows_vmem.at[pl.ds(unit * width, width)], load_sem.at[unit]
        ).start()

    batch_units = BATCH // width
    for group in range(n_groups):
        for half in (other, core):
            for k in range(batch_units):
                unit = (half * n_groups + group) * batch_units + k
                if group < n_groups - 1 or k < batch_units - 1:
                    load(following_ref.at[pl.ds(unit * width, width)], unit)
                    continue

                @pl.when(half == 1)
                def _():
                    load(panel_ref, units - 1)

                @pl.when(half == 0)
                def _():
                    load(following_ref.at[pl.ds((units // 2 - 1) * width, width)], units // 2 - 1)

    barrier = pltpu.get_barrier_semaphore()
    n_signals = 0
    for k in range(1, n_chips):
        pl.semaphore_signal(
            barrier, inc=1, device_id=chip_device(lax.rem(chip + k, n_chips)), device_id_type=MESH
        )
        n_signals += 1
    for k in range(1, n_gy, 2):
        pl.semaphore_signal(
            barrier, inc=1, device_id=(me_x, lax.rem(me_y + k, n_gy)), device_id_type=MESH
        )
        n_signals += 1

    load_panel.wait()
    high, low = halves(panel_vmem[...])
    panel_split[0:width, :] = high
    panel_split[width : 2 * width, :] = low
    quads = rows_product(panel_split[...], panel_split[...])
    pair = quads[:width] + quads[width:]
    gram = pair[:, :width] + pair[:, width:]
    gram_own[...] = jnp.concatenate([gram[: width // 2], gram[width // 2 :]], axis=1)

    pl.semaphore_wait(barrier, n_signals)

    gy_copies = []
    for k in range(1, n_gy):
        copy = pltpu.make_async_remote_copy(
            src_ref=gram_own,
            dst_ref=gram_gy.at[k - 1],
            send_sem=gy_send.at[k - 1],
            recv_sem=gy_recv.at[k - 1],
            device_id=(me_x, lax.rem(me_y + k, n_gy)),
            device_id_type=MESH,
        )
        copy.start()
        gy_copies.append(copy)

    def cross(half, group):
        index = half * n_groups + group
        for k in range(batch_units):
            unit = index * batch_units + k
            pltpu.make_async_copy(
                panel_ref, rows_vmem.at[pl.ds(unit * width, width)], load_sem.at[unit]
            ).wait()
        row_high, row_low = halves(rows_vmem[pl.ds(index * BATCH, BATCH), :])
        quads = rows_product(jnp.concatenate([row_high, row_low], axis=0), panel_split[...])
        pair = quads[:BATCH] + quads[BATCH:]
        for k in range(BATCH // LANES):
            turned = pair[k * LANES : (k + 1) * LANES].T
            part[pl.ds(index * group_rows + k * width, width), :] = turned[:width] + turned[width:]

    half_copies, rs_copies, ag_copies, back_copies = [], [], [], []

    def start_half(group):
        copy = pltpu.make_async_remote_copy(
            src_ref=part.at[pl.ds(other * half_rows + group * group_rows, group_rows)],
            dst_ref=half_in.at[pl.ds(group * group_rows, group_rows)],
            send_sem=half_send.at[group],
            recv_sem=half_recv.at[group],
            device_id=sibling,
            device_id_type=MESH,
        )
        copy.start()
        half_copies.append(copy)

    def start_scatter(group):
        half_copies[group].wait_recv()
        start = group * group_rows
        half_sum[start : start + group_rows, :] = (
            part[pl.ds(core * half_rows + start, group_rows), :]
            + half_in[start : start + group_rows, :]
        )
        copies = []
        for k in range(1, n_chips):
            to = lax.rem(chip + k, n_chips)
            copy = pltpu.make_async_remote_copy(
                src_ref=half_sum.at[pl.ds(start + to * piece, piece)],
                dst_ref=piece_in.at[group, k - 1],
                send_sem=rs_send.at[group, k - 1],
                recv_sem=rs_recv.at[group, k - 1],
                device_id=chip_device(to),
                device_id_type=MESH,
            )
            copy.start()
            copies.append(copy)
        rs_copies.append(copies)

    def start_gather(group):
        for copy in rs_copies[group]:
            copy.wait_recv()
        own = half_sum[pl.ds(group * group_rows + chip * piece, piece), :]
        for k in range(n_chips - 1):
            own = own + piece_in[group, k]
        start = core * half_rows + group * group_rows + chip * piece
        total[pl.ds(start, piece), :] = own
        copies = []
        for k in range(1, n_chips):
            copy = pltpu.make_async_remote_copy(
                src_ref=total.at[pl.ds(start, piece)],
                dst_ref=total.at[pl.ds(start, piece)],
                send_sem=ag_send.at[group, k - 1],
                recv_sem=ag_recv.at[group, k - 1],
                device_id=chip_device(lax.rem(chip + k, n_chips)),
                device_id_type=MESH,
            )
            copy.start()
            copies.append(copy)
        ag_copies.append(copies)

    def start_back(group):
        for copy in ag_copies[group]:
            copy.wait_recv()
        start = core * half_rows + group * group_rows
        copy = pltpu.make_async_remote_copy(
            src_ref=total.at[pl.ds(start, group_rows)],
            dst_ref=total.at[pl.ds(start, group_rows)],
            send_sem=back_send.at[group],
            recv_sem=back_recv.at[group],
            device_id=sibling,
            device_id_type=MESH,
        )
        copy.start()
        back_copies.append(copy)

    gx_copies = []
    for group in range(n_groups):
        cross(other, group)
        start_half(group)
        if group == 0:
            for copy in gy_copies:
                copy.wait_recv()
            gram_mid[...] = ordered_sum(gram_own, gram_gy, me_y, n_gy)
            for k in range(1, n_gx):
                copy = pltpu.make_async_remote_copy(
                    src_ref=gram_mid,
                    dst_ref=gram_gx.at[k - 1],
                    send_sem=gx_send.at[k - 1],
                    recv_sem=gx_recv.at[k - 1],
                    device_id=(lax.rem(me_x + k, n_gx), me_y),
                    device_id_type=MESH,
                )
                copy.start()
                gx_copies.append(copy)
        cross(core, group)
        start_scatter(group)
    for group in range(n_groups - 1):
        start_gather(group)

    for copy in gx_copies:
        copy.wait_recv()
    packed = ordered_sum(gram_mid, gram_gx, me_x, n_gx)
    eliminate(jnp.concatenate([packed[:, :width], packed[:, width:]], axis=0), wide_ref)
    start_gather(n_groups - 1)

    stacked = write_upper(root_rows, wide_ref, upper_ref)
    write_basis(root_rows, stacked, panel_vmem, basis_vmem)
    store = pltpu.make_async_copy(basis_vmem, basis_ref, store_sem)
    store.start()
    for group in range(n_groups):
        start_back(group)
    for group in range(n_groups):
        back_copies[group].wait_recv()
        for half in range(2):
            for k in range(BATCH // LANES):
                block = (half * n_groups + group) * (BATCH // LANES) + k
                write_projection(root_rows, stacked, total, proj_ref, block)
    store.wait()
    for copies in rs_copies + ag_copies + [gy_copies, gx_copies, half_copies, back_copies]:
        for copy in copies:
            copy.wait_send()


def exchanged(panel, following, n_gx, n_gy, root_rows):
    width, cells = panel.shape
    rows = width + following.shape[0]
    all_rows = rows // LANES * width
    half_rows = all_rows // 2
    group_rows = BATCH // LANES * width
    n_groups = half_rows // group_rows
    n_chips = n_gx * n_gy // 2
    piece = group_rows // n_chips
    gram_block = (width // 2, 2 * width)
    dma = pltpu.SemaphoreType.DMA
    f32 = jnp.float32
    return pl.pallas_call(
        functools.partial(sum_kernel, n_gx, n_gy, root_rows),
        out_shape=(
            jax.ShapeDtypeStruct((width, cells), f32),
            jax.ShapeDtypeStruct((width, width), f32),
            jax.ShapeDtypeStruct((width, following.shape[0]), f32),
        ),
        in_specs=[pl.BlockSpec(memory_space=pltpu.HBM)] * 2,
        out_specs=(
            pl.BlockSpec(memory_space=pl.ANY),
            pl.BlockSpec(memory_space=pltpu.VMEM),
            pl.BlockSpec(memory_space=pltpu.VMEM),
        ),
        scratch_shapes=[
            pltpu.VMEM((width, 2 * width), f32),
            pltpu.VMEM((width, cells), f32),
            pltpu.VMEM((width, cells), f32),
            pltpu.VMEM((rows, cells), f32),
            pltpu.VMEM((2 * width, cells), jnp.bfloat16),
            pltpu.VMEM((all_rows, LANES), f32),
            pltpu.VMEM(gram_block, f32),
            pltpu.VMEM((n_gy - 1,) + gram_block, f32),
            pltpu.VMEM(gram_block, f32),
            pltpu.VMEM((n_gx - 1,) + gram_block, f32),
            pltpu.VMEM((half_rows, LANES), f32),
            pltpu.VMEM((half_rows, LANES), f32),
            pltpu.VMEM((n_groups, n_chips - 1, piece, LANES), f32),
            pltpu.VMEM((all_rows, LANES), f32),
            dma,
            dma,
            dma((rows // width,)),
            dma((n_gy - 1,)),
            dma((n_gy - 1,)),
            dma((n_gx - 1,)),
            dma((n_gx - 1,)),
            dma((n_groups,)),
            dma((n_groups,)),
            dma((n_groups, n_chips - 1)),
            dma((n_groups, n_chips - 1)),
            dma((n_groups, n_chips - 1)),
            dma((n_groups, n_chips - 1)),
            dma((n_groups,)),
            dma((n_groups,)),
        ],
        compiler_params=pltpu.CompilerParams(
            collective_id=0, has_side_effects=True, vmem_limit_bytes=56 * 2**20
        ),
        name="sum_and_factor",
    )(panel, following)


def apply_kernel(root_rows, sums_ref, wide_ref, panel_ref, basis_ref, upper_ref, proj_ref):
    stacked = write_upper(root_rows, wide_ref, upper_ref)
    for block in range(sums_ref.shape[0] // panel_ref.shape[0]):
        write_projection(root_rows, stacked, sums_ref, proj_ref, block)
    write_basis(root_rows, stacked, panel_ref, basis_ref)


def applied(sums, wide, panel, next_count, root_rows):
    width, cells = panel.shape
    f32 = jnp.float32
    return pl.pallas_call(
        functools.partial(apply_kernel, root_rows),
        out_shape=(
            jax.ShapeDtypeStruct((width, cells), f32),
            jax.ShapeDtypeStruct((width, width), f32),
            jax.ShapeDtypeStruct((width, next_count), f32),
        ),
        compiler_params=pltpu.CompilerParams(vmem_limit_bytes=60 * 2**20),
        name="apply_factor",
    )(sums, wide, panel)


def plain_sums(panel, following):
    precise = functools.partial(
        lax.dot_general,
        dimension_numbers=(((1,), (1,)), ((), ())),
        precision=lax.Precision.HIGHEST,
        preferred_element_type=jnp.float32,
    )
    width = panel.shape[0]
    cross = lax.psum(
        jnp.concatenate([precise(panel, following), precise(panel, panel)], axis=1), ("gx", "gy")
    )
    blocks = cross.shape[1] // LANES
    sums = cross.reshape(width, blocks, LANES).transpose(1, 0, 2).reshape(blocks * width, LANES)
    wide = pl.pallas_call(
        lambda gram_ref, wide_ref: eliminate(gram_ref[...], wide_ref),
        out_shape=jax.ShapeDtypeStruct((width, 2 * width), jnp.float32),
        name="factor",
    )(cross[:, -width:])
    return sums, wide


def body(n_gx, n_gy, panel, following):
    width, cells = panel.shape
    root_rows = math.sqrt(cells * n_gx * n_gy)
    if BATCH // LANES * width % (8 * (n_gx * n_gy // 2)) == 0:
        return exchanged(panel, following, n_gx, n_gy, root_rows)
    sums, wide = plain_sums(panel, following)
    return applied(sums, wide, panel, following.shape[0], root_rows)


def solution(mesh):
    return jax.shard_map(
        functools.partial(body, mesh.shape["gx"], mesh.shape["gy"]),
        mesh=mesh,
        in_specs=(P(None, ("gx", "gy")), P(None, ("gx", "gy"))),
        out_specs=(P(None, ("gx", "gy")), P(), P()),
        check_vma=False,
    )
```

time: 28.6 us -> 33 us (1.15); the launches traced: 28.5 us -> 32.6 us
  local copies, waits for them, and re-layouts: 0 us -> 4.92 us
  Pallas kernels: 27.9 us -> 27 us
    unnamed x0 -> x3, local copies, waits for them, and re-layouts: none -> 4.92 us
    pallas_call x2 -> x1, Pallas kernels: 27.9 us -> 27 us  [exchanged(): pl.pallas_call(functools.partial(sum_kernel, n_gx, n_gy, root_rows), out_...]
where the time goes in v4:
time: 33 us; the launch traced here: 32.6 us
  Pallas kernels  27 us (82%)
  local copies, waits for them, and re-layouts  4.92 us (15%)
  between operations  0.64 us (2%)
    pallas_call x1, Pallas kernels, exchanged(): pl.pallas_call(functools.partial(sum_kernel, n_gx, n_gy, root_rows), out_...  27 us
    unnamed x3, local copies, waits for them, and re-layouts  4.92 us

profile of v4, /device:TPU:0, one launch (start us, length us, event | category | flops | bytes accessed | tf_op | source)
XLA Modules:
  0.0 32.6 jit_solution(11596800268312285450)
XLA Ops:
  0.6 27.0 %sum_and_factor.1 = (f32[64,2048]{1,0:T(8,128)}, f32[64,64]{1,0:T(8,128)}, f32[64,960]{1,0:T(8,128)}) custom-call(f32[64,2048]{1,0:T(8,128)} %panel_ref.1, f32[960,2048]{1,0:T(8,128)} %following_ref.1), custom_call_target="tpu_custom_call" | custom-call | tf_op jit(solution)/shard_map/sum_and_factor/pallas_call | solution.py:370
  27.6 1.9 %copy.8 = f32[64,2048]{1,0:T(8,128)} copy(f32[64,2048]{1,0:T(8,128)} %get-tuple-element.6) | data formatting | bytes 1048576
  29.5 1.4 %copy.9 = f32[64,64]{1,0:T(8,128)} copy(f32[64,64]{1,0:T(8,128)} %get-tuple-element.7) | data formatting | bytes 32768
  30.9 1.7 %copy.10 = f32[64,960]{1,0:T(8,128)} copy(f32[64,960]{1,0:T(8,128)} %get-tuple-element.8) | data formatting | bytes 491520

commit v5 on v4

--- a/solution.py
+++ b/solution.py
@@ -11,6 +11,7 @@
 MESH = pl.DeviceIdType.MESH
 LANES = 128
 BATCH = 256
+CELLS = 512
 
 
 def halves(values):
@@ -18,10 +19,8 @@
     return high, (values - high.astype(jnp.float32)).astype(jnp.bfloat16)
 
 
-def rows_product(left, right):
-    return lax.dot_general(
-        left, right, (((1,), (1,)), ((), ())), preferred_element_type=jnp.float32
-    )
+def product(left, right):
+    return jnp.dot(left, right, preferred_element_type=jnp.float32)
 
 
 def eliminate(gram, out_ref):
@@ -106,17 +105,13 @@
 def sum_kernel(
     n_gx,
     n_gy,
-    root_rows,
     panel_ref,
     following_ref,
-    basis_ref,
-    upper_ref,
-    proj_ref,
+    sums_ref,
     wide_ref,
-    basis_vmem,
     panel_vmem,
     rows_vmem,
-    panel_split,
+    panel_turned,
     part,
     gram_own,
     gram_gy,
@@ -127,7 +122,6 @@
     piece_in,
     total,
     load_panel_sem,
-    store_sem,
     load_sem,
     gy_send,
     gy_recv,
@@ -197,10 +191,11 @@
         n_signals += 1
 
     load_panel.wait()
-    high, low = halves(panel_vmem[...])
-    panel_split[0:width, :] = high
-    panel_split[width : 2 * width, :] = low
-    quads = rows_product(panel_split[...], panel_split[...])
+    panel = panel_vmem[...]
+    high = panel.astype(jnp.bfloat16).astype(jnp.float32)
+    split = jnp.concatenate([high, panel - high], axis=0)
+    panel_turned[...] = split.T.astype(jnp.bfloat16)
+    quads = product(split.astype(jnp.bfloat16), panel_turned[...])
     pair = quads[:width] + quads[width:]
     gram = pair[:, :width] + pair[:, width:]
     gram_own[...] = jnp.concatenate([gram[: width // 2], gram[width // 2 :]], axis=1)
@@ -227,9 +222,13 @@
             pltpu.make_async_copy(
                 panel_ref, rows_vmem.at[pl.ds(unit * width, width)], load_sem.at[unit]
             ).wait()
-        row_high, row_low = halves(rows_vmem[pl.ds(index * BATCH, BATCH), :])
-        quads = rows_product(jnp.concatenate([row_high, row_low], axis=0), panel_split[...])
-        pair = quads[:BATCH] + quads[BATCH:]
+        pair = jnp.zeros((BATCH, 2 * width), jnp.float32)
+        for start in range(0, rows_vmem.shape[1], CELLS):
+            rows = rows_vmem[pl.ds(index * BATCH, BATCH), start : start + CELLS]
+            quads = product(
+                jnp.concatenate(halves(rows), axis=0), panel_turned[start : start + CELLS, :]
+            )
+            pair = pair + (quads[:BATCH] + quads[BATCH:])
         for k in range(BATCH // LANES):
             turned = pair[k * LANES : (k + 1) * LANES].T
             part[pl.ds(index * group_rows + k * width, width), :] = turned[:width] + turned[width:]
@@ -337,25 +336,17 @@
     eliminate(jnp.concatenate([packed[:, :width], packed[:, width:]], axis=0), wide_ref)
     start_gather(n_groups - 1)
 
-    stacked = write_upper(root_rows, wide_ref, upper_ref)
-    write_basis(root_rows, stacked, panel_vmem, basis_vmem)
-    store = pltpu.make_async_copy(basis_vmem, basis_ref, store_sem)
-    store.start()
     for group in range(n_groups):
         start_back(group)
-    for group in range(n_groups):
-        back_copies[group].wait_recv()
-        for half in range(2):
-            for k in range(BATCH // LANES):
-                block = (half * n_groups + group) * (BATCH // LANES) + k
-                write_projection(root_rows, stacked, total, proj_ref, block)
-    store.wait()
+    for copy in back_copies:
+        copy.wait_recv()
+    sums_ref[...] = total[...]
     for copies in rs_copies + ag_copies + [gy_copies, gx_copies, half_copies, back_copies]:
         for copy in copies:
             copy.wait_send()
 
 
-def exchanged(panel, following, n_gx, n_gy, root_rows):
+def exchanged(panel, following, n_gx, n_gy):
     width, cells = panel.shape
     rows = width + following.shape[0]
     all_rows = rows // LANES * width
@@ -368,24 +359,20 @@
     dma = pltpu.SemaphoreType.DMA
     f32 = jnp.float32
     return pl.pallas_call(
-        functools.partial(sum_kernel, n_gx, n_gy, root_rows),
+        functools.partial(sum_kernel, n_gx, n_gy),
         out_shape=(
-            jax.ShapeDtypeStruct((width, cells), f32),
-            jax.ShapeDtypeStruct((width, width), f32),
-            jax.ShapeDtypeStruct((width, following.shape[0]), f32),
+            jax.ShapeDtypeStruct((all_rows, LANES), f32),
+            jax.ShapeDtypeStruct((width, 2 * width), f32),
         ),
         in_specs=[pl.BlockSpec(memory_space=pltpu.HBM)] * 2,
         out_specs=(
-            pl.BlockSpec(memory_space=pl.ANY),
             pl.BlockSpec(memory_space=pltpu.VMEM),
             pl.BlockSpec(memory_space=pltpu.VMEM),
         ),
         scratch_shapes=[
-            pltpu.VMEM((width, 2 * width), f32),
-            pltpu.VMEM((width, cells), f32),
             pltpu.VMEM((width, cells), f32),
             pltpu.VMEM((rows, cells), f32),
-            pltpu.VMEM((2 * width, cells), jnp.bfloat16),
+            pltpu.VMEM((cells, 2 * width), jnp.bfloat16),
             pltpu.VMEM((all_rows, LANES), f32),
             pltpu.VMEM(gram_block, f32),
             pltpu.VMEM((n_gy - 1,) + gram_block, f32),
@@ -395,7 +382,6 @@
             pltpu.VMEM((half_rows, LANES), f32),
             pltpu.VMEM((n_groups, n_chips - 1, piece, LANES), f32),
             pltpu.VMEM((all_rows, LANES), f32),
-            dma,
             dma,
             dma((rows // width,)),
             dma((n_gy - 1,)),
@@ -465,8 +451,9 @@
     width, cells = panel.shape
     root_rows = math.sqrt(cells * n_gx * n_gy)
     if BATCH // LANES * width % (8 * (n_gx * n_gy // 2)) == 0:
-        return exchanged(panel, following, n_gx, n_gy, root_rows)
-    sums, wide = plain_sums(panel, following)
+        sums, wide = exchanged(panel, following, n_gx, n_gy)
+    else:
+        sums, wide = plain_sums(panel, following)
     return applied(sums, wide, panel, following.shape[0], root_rows)
 
 

time: 33 us -> 30.3 us (0.918)
  local copies, waits for them, and re-layouts: 4.92 us -> 0 us
  Pallas kernels: 27 us -> 29.4 us
    unnamed x3 -> x0, local copies, waits for them, and re-layouts: 4.92 us -> none
    pallas_call x1 -> x2, Pallas kernels: 27 us -> 29.4 us  [the longest x1 27 us: exchanged(): pl.pallas_call(functools.partial(sum_kernel, n_gx, n_gy), out_shape=(jax....]
where the time goes in v5:
time: 30.3 us; the launch traced here: 30.1 us
  Pallas kernels  29.4 us (97%)
  between operations  0.64 us (2%)
    pallas_call x1, Pallas kernels, exchanged(): pl.pallas_call(functools.partial(sum_kernel, n_gx, n_gy), out_shape=(jax....  27 us
    pallas_call x1, Pallas kernels, applied(): pl.pallas_call(functools.partial(apply_kernel, root_rows), out_shape=(jax...  2.4 us

profile of v5, /device:TPU:0, one launch (start us, length us, event | category | flops | bytes accessed | tf_op | source)
XLA Modules:
  0.0 30.1 jit_solution(10026835932977157759)
XLA Ops:
  0.6 27.0 %sum_and_factor.1 = (f32[512,128]{1,0:T(8,128)}, f32[64,128]{1,0:T(8,128)}) custom-call(f32[64,2048]{1,0:T(8,128)} %panel_ref.3, f32[960,2048]{1,0:T(8,128)} %following_ref.1), custom_call_target="tpu_custom_call" | custom-call | tf_op jit(solution)/shard_map/sum_and_factor/pallas_call | solution.py:361
  27.7 2.4 %apply_factor.1 = (f32[64,2048]{1,0:T(8,128)}, f32[64,64]{1,0:T(8,128)}, f32[64,960]{1,0:T(8,128)}) custom-call(f32[512,128]{1,0:T(8,128)} %get-tuple-element.5.sums_ref, f32[64,128]{1,0:T(8,128)} %get-tuple-element.6.wide_ref, f32[64,2048]{1,0:T(8,128)} %panel_ref.3), custom_call_target="tpu_custom_call" | custom-call | tf_op jit(solution)/shard_map/apply_factor/pallas_call | solution.py:417

commit v6 on v5

--- a/solution.py
+++ b/solution.py
@@ -138,11 +138,11 @@
 ):
     width = panel_ref.shape[0]
     units = rows_vmem.shape[0] // width
-    half_rows = rows_vmem.shape[0] // LANES * width // 2
-    group_rows = BATCH // LANES * width
-    n_groups = half_rows // group_rows
+    half_batches = rows_vmem.shape[0] // BATCH // 2
+    batch_rows = BATCH // LANES * width
+    half_rows = half_batches * batch_rows
     n_chips = n_gx * n_gy // 2
-    piece = group_rows // n_chips
+    piece = half_rows // n_chips
     me_x, me_y = lax.axis_index("gx"), lax.axis_index("gy")
     core = lax.rem(me_y, 2)
     other = 1 - core
@@ -155,40 +155,36 @@
     load_panel = pltpu.make_async_copy(panel_ref, panel_vmem, load_panel_sem)
     load_panel.start()
 
-    def load(source, unit):
-        pltpu.make_async_copy(
-            source, rows_vmem.at[pl.ds(unit * width, width)], load_sem.at[unit]
-        ).start()
-
-    batch_units = BATCH // width
-    for group in range(n_groups):
-        for half in (other, core):
-            for k in range(batch_units):
-                unit = (half * n_groups + group) * batch_units + k
-                if group < n_groups - 1 or k < batch_units - 1:
-                    load(following_ref.at[pl.ds(unit * width, width)], unit)
-                    continue
-
-                @pl.when(half == 1)
-                def _():
-                    load(panel_ref, units - 1)
-
-                @pl.when(half == 0)
-                def _():
-                    load(following_ref.at[pl.ds((units // 2 - 1) * width, width)], units // 2 - 1)
+    @pl.loop(0, units)
+    def _(step):
+        unit = lax.rem(step + other * (units // 2), units)
+
+        def load(source):
+            pltpu.make_async_copy(
+                source, rows_vmem.at[pl.ds(unit * width, width)], load_sem.at[unit]
+            ).start()
+
+        @pl.when(unit == units - 1)
+        def _():
+            load(panel_ref)
+
+        @pl.when(unit != units - 1)
+        def _():
+            load(following_ref.at[pl.ds(unit * width, width)])
 
     barrier = pltpu.get_barrier_semaphore()
-    n_signals = 0
-    for k in range(1, n_chips):
+
+    @pl.loop(1, n_chips)
+    def _(k):
         pl.semaphore_signal(
             barrier, inc=1, device_id=chip_device(lax.rem(chip + k, n_chips)), device_id_type=MESH
         )
-        n_signals += 1
+
     for k in range(1, n_gy, 2):
         pl.semaphore_signal(
             barrier, inc=1, device_id=(me_x, lax.rem(me_y + k, n_gy)), device_id_type=MESH
         )
-        n_signals += 1
+    n_signals = n_chips - 1 + n_gy // 2
 
     load_panel.wait()
     panel = panel_vmem[...]
@@ -202,9 +198,8 @@
 
     pl.semaphore_wait(barrier, n_signals)
 
-    gy_copies = []
-    for k in range(1, n_gy):
-        copy = pltpu.make_async_remote_copy(
+    def gy_copy(k):
+        return pltpu.make_async_remote_copy(
             src_ref=gram_own,
             dst_ref=gram_gy.at[k - 1],
             send_sem=gy_send.at[k - 1],
@@ -212,13 +207,77 @@
             device_id=(me_x, lax.rem(me_y + k, n_gy)),
             device_id_type=MESH,
         )
-        copy.start()
-        gy_copies.append(copy)
-
-    def cross(half, group):
-        index = half * n_groups + group
-        for k in range(batch_units):
-            unit = index * batch_units + k
+
+    def gx_copy(k):
+        return pltpu.make_async_remote_copy(
+            src_ref=gram_mid,
+            dst_ref=gram_gx.at[k - 1],
+            send_sem=gx_send.at[k - 1],
+            recv_sem=gx_recv.at[k - 1],
+            device_id=(lax.rem(me_x + k, n_gx), me_y),
+            device_id_type=MESH,
+        )
+
+    def half_copy():
+        return pltpu.make_async_remote_copy(
+            src_ref=part.at[pl.ds(other * half_rows, half_rows)],
+            dst_ref=half_in,
+            send_sem=half_send,
+            recv_sem=half_recv,
+            device_id=sibling,
+            device_id_type=MESH,
+        )
+
+    def scatter_copy(k):
+        to = lax.rem(chip + k, n_chips)
+        return pltpu.make_async_remote_copy(
+            src_ref=half_sum.at[pl.ds(to * piece, piece)],
+            dst_ref=piece_in.at[k - 1],
+            send_sem=rs_send.at[k - 1],
+            recv_sem=rs_recv.at[k - 1],
+            device_id=chip_device(to),
+            device_id_type=MESH,
+        )
+
+    own_start = core * half_rows + chip * piece
+
+    def gather_copy(k):
+        return pltpu.make_async_remote_copy(
+            src_ref=total.at[pl.ds(own_start, piece)],
+            dst_ref=total.at[pl.ds(own_start, piece)],
+            send_sem=ag_send.at[k - 1],
+            recv_sem=ag_recv.at[k - 1],
+            device_id=chip_device(lax.rem(chip + k, n_chips)),
+            device_id_type=MESH,
+        )
+
+    def back_copy():
+        return pltpu.make_async_remote_copy(
+            src_ref=total.at[pl.ds(core * half_rows, half_rows)],
+            dst_ref=total.at[pl.ds(core * half_rows, half_rows)],
+            send_sem=back_send,
+            recv_sem=back_recv,
+            device_id=sibling,
+            device_id_type=MESH,
+        )
+
+    def start_all(copy, count):
+        pl.loop(1, count)(lambda k: copy(k).start())
+
+    def receive_all(copy, count):
+        pl.loop(1, count)(lambda k: copy(k).wait_recv())
+
+    def sent_all(copy, count):
+        pl.loop(1, count)(lambda k: copy(k).wait_send())
+
+    start_all(gy_copy, n_gy)
+
+    @pl.loop(0, 2 * half_batches)
+    def _(step):
+        half = lax.rem(other + step // half_batches, 2)
+        index = half * half_batches + lax.rem(step, half_batches)
+        for k in range(BATCH // width):
+            unit = index * (BATCH // width) + k
             pltpu.make_async_copy(
                 panel_ref, rows_vmem.at[pl.ds(unit * width, width)], load_sem.at[unit]
             ).wait()
@@ -231,119 +290,39 @@
             pair = pair + (quads[:BATCH] + quads[BATCH:])
         for k in range(BATCH // LANES):
             turned = pair[k * LANES : (k + 1) * LANES].T
-            part[pl.ds(index * group_rows + k * width, width), :] = turned[:width] + turned[width:]
-
-    half_copies, rs_copies, ag_copies, back_copies = [], [], [], []
-
-    def start_half(group):
-        copy = pltpu.make_async_remote_copy(
-            src_ref=part.at[pl.ds(other * half_rows + group * group_rows, group_rows)],
-            dst_ref=half_in.at[pl.ds(group * group_rows, group_rows)],
-            send_sem=half_send.at[group],
-            recv_sem=half_recv.at[group],
-            device_id=sibling,
-            device_id_type=MESH,
-        )
-        copy.start()
-        half_copies.append(copy)
-
-    def start_scatter(group):
-        half_copies[group].wait_recv()
-        start = group * group_rows
-        half_sum[start : start + group_rows, :] = (
-            part[pl.ds(core * half_rows + start, group_rows), :]
-            + half_in[start : start + group_rows, :]
-        )
-        copies = []
-        for k in range(1, n_chips):
-            to = lax.rem(chip + k, n_chips)
-            copy = pltpu.make_async_remote_copy(
-                src_ref=half_sum.at[pl.ds(start + to * piece, piece)],
-                dst_ref=piece_in.at[group, k - 1],
-                send_sem=rs_send.at[group, k - 1],
-                recv_sem=rs_recv.at[group, k - 1],
-                device_id=chip_device(to),
-                device_id_type=MESH,
-            )
-            copy.start()
-            copies.append(copy)
-        rs_copies.append(copies)
-
-    def start_gather(group):
-        for copy in rs_copies[group]:
-            copy.wait_recv()
-        own = half_sum[pl.ds(group * group_rows + chip * piece, piece), :]
-        for k in range(n_chips - 1):
-            own = own + piece_in[group, k]
-        start = core * half_rows + group * group_rows + chip * piece
-        total[pl.ds(start, piece), :] = own
-        copies = []
-        for k in range(1, n_chips):
-            copy = pltpu.make_async_remote_copy(
-                src_ref=total.at[pl.ds(start, piece)],
-                dst_ref=total.at[pl.ds(start, piece)],
-                send_sem=ag_send.at[group, k - 1],
-                recv_sem=ag_recv.at[group, k - 1],
-                device_id=chip_device(lax.rem(chip + k, n_chips)),
-                device_id_type=MESH,
-            )
-            copy.start()
-            copies.append(copy)
-        ag_copies.append(copies)
-
-    def start_back(group):
-        for copy in ag_copies[group]:
-            copy.wait_recv()
-        start = core * half_rows + group * group_rows
-        copy = pltpu.make_async_remote_copy(
-            src_ref=total.at[pl.ds(start, group_rows)],
-            dst_ref=total.at[pl.ds(start, group_rows)],
-            send_sem=back_send.at[group],
-            recv_sem=back_recv.at[group],
-            device_id=sibling,
-            device_id_type=MESH,
-        )
-        copy.start()
-        back_copies.append(copy)
-
-    gx_copies = []
-    for group in range(n_groups):
-        cross(other, group)
-        start_half(group)
-        if group == 0:
-            for copy in gy_copies:
-                copy.wait_recv()
+            part[pl.ds(index * batch_rows + k * width, width), :] = turned[:width] + turned[width:]
+
+        @pl.when(step == half_batches - 1)
+        def _():
+            half_copy().start()
+            receive_all(gy_copy, n_gy)
             gram_mid[...] = ordered_sum(gram_own, gram_gy, me_y, n_gy)
-            for k in range(1, n_gx):
-                copy = pltpu.make_async_remote_copy(
-                    src_ref=gram_mid,
-                    dst_ref=gram_gx.at[k - 1],
-                    send_sem=gx_send.at[k - 1],
-                    recv_sem=gx_recv.at[k - 1],
-                    device_id=(lax.rem(me_x + k, n_gx), me_y),
-                    device_id_type=MESH,
-                )
-                copy.start()
-                gx_copies.append(copy)
-        cross(core, group)
-        start_scatter(group)
-    for group in range(n_groups - 1):
-        start_gather(group)
-
-    for copy in gx_copies:
-        copy.wait_recv()
+            start_all(gx_copy, n_gx)
+
+    half_copy().wait_recv()
+    half_sum[...] = part[pl.ds(core * half_rows, half_rows), :] + half_in[...]
+    start_all(scatter_copy, n_chips)
+
+    receive_all(gx_copy, n_gx)
     packed = ordered_sum(gram_mid, gram_gx, me_x, n_gx)
     eliminate(jnp.concatenate([packed[:, :width], packed[:, width:]], axis=0), wide_ref)
-    start_gather(n_groups - 1)
-
-    for group in range(n_groups):
-        start_back(group)
-    for copy in back_copies:
-        copy.wait_recv()
+
+    receive_all(scatter_copy, n_chips)
+    own = half_sum[pl.ds(chip * piece, piece), :]
+    for k in range(n_chips - 1):
+        own = own + piece_in[k]
+    total[pl.ds(own_start, piece), :] = own
+    start_all(gather_copy, n_chips)
+    sent_all(gy_copy, n_gy)
+    sent_all(gx_copy, n_gx)
+    half_copy().wait_send()
+    sent_all(scatter_copy, n_chips)
+    receive_all(gather_copy, n_chips)
+    back_copy().start()
+    sent_all(gather_copy, n_chips)
+    back_copy().wait_recv()
     sums_ref[...] = total[...]
-    for copies in rs_copies + ag_copies + [gy_copies, gx_copies, half_copies, back_copies]:
-        for copy in copies:
-            copy.wait_send()
+    back_copy().wait_send()
 
 
 def exchanged(panel, following, n_gx, n_gy):
@@ -351,10 +330,8 @@
     rows = width + following.shape[0]
     all_rows = rows // LANES * width
     half_rows = all_rows // 2
-    group_rows = BATCH // LANES * width
-    n_groups = half_rows // group_rows
     n_chips = n_gx * n_gy // 2
-    piece = group_rows // n_chips
+    piece = half_rows // n_chips
     gram_block = (width // 2, 2 * width)
     dma = pltpu.SemaphoreType.DMA
     f32 = jnp.float32
@@ -380,7 +357,7 @@
             pltpu.VMEM((n_gx - 1,) + gram_block, f32),
             pltpu.VMEM((half_rows, LANES), f32),
             pltpu.VMEM((half_rows, LANES), f32),
-            pltpu.VMEM((n_groups, n_chips - 1, piece, LANES), f32),
+            pltpu.VMEM((n_chips - 1, piece, LANES), f32),
             pltpu.VMEM((all_rows, LANES), f32),
             dma,
             dma((rows // width,)),
@@ -388,14 +365,14 @@
             dma((n_gy - 1,)),
             dma((n_gx - 1,)),
             dma((n_gx - 1,)),
-            dma((n_groups,)),
-            dma((n_groups,)),
-            dma((n_groups, n_chips - 1)),
-            dma((n_groups, n_chips - 1)),
-            dma((n_groups, n_chips - 1)),
-            dma((n_groups, n_chips - 1)),
-            dma((n_groups,)),
-            dma((n_groups,)),
+            dma,
+            dma,
+            dma((n_chips - 1,)),
+            dma((n_chips - 1,)),
+            dma((n_chips - 1,)),
+            dma((n_chips - 1,)),
+            dma,
+            dma,
         ],
         compiler_params=pltpu.CompilerParams(
             collective_id=0, has_side_effects=True, vmem_limit_bytes=56 * 2**20
@@ -450,7 +427,8 @@
 def body(n_gx, n_gy, panel, following):
     width, cells = panel.shape
     root_rows = math.sqrt(cells * n_gx * n_gy)
-    if BATCH // LANES * width % (8 * (n_gx * n_gy // 2)) == 0:
+    half_rows = (width + following.shape[0]) // LANES * width // 2
+    if half_rows % (8 * (n_gx * n_gy // 2)) == 0:
         sums, wide = exchanged(panel, following, n_gx, n_gy)
     else:
         sums, wide = plain_sums(panel, following)

time: 30.3 us -> 28.4 us (0.937)
  Pallas kernels: 29.4 us -> 27.7 us
    pallas_call x1, Pallas kernels: 27 us -> 25.3 us  [exchanged(): pl.pallas_call(functools.partial(sum_kernel, n_gx, n_gy), out_shape=(jax....]
where the time goes in v6:
time: 28.4 us; the launch traced here: 28.3 us
  Pallas kernels  27.7 us (98%)
  between operations  0.64 us (2%)
    pallas_call x1, Pallas kernels, exchanged(): pl.pallas_call(functools.partial(sum_kernel, n_gx, n_gy), out_shape=(jax....  25.3 us
    pallas_call x1, Pallas kernels, applied(): pl.pallas_call(functools.partial(apply_kernel, root_rows), out_shape=(jax...  2.4 us

profile of v6, /device:TPU:0, one launch (start us, length us, event | category | flops | bytes accessed | tf_op | source)
XLA Modules:
  0.0 28.3 jit_solution(15701861018402188441)
XLA Ops:
  0.6 25.3 %sum_and_factor.1 = (f32[512,128]{1,0:T(8,128)}, f32[64,128]{1,0:T(8,128)}) custom-call(f32[64,2048]{1,0:T(8,128)} %panel_ref.3, f32[960,2048]{1,0:T(8,128)} %following_ref.1), custom_call_target="tpu_custom_call" | custom-call | tf_op jit(solution)/shard_map/sum_and_factor/pallas_call | solution.py:338
  25.9 2.4 %apply_factor.1 = (f32[64,2048]{1,0:T(8,128)}, f32[64,64]{1,0:T(8,128)}, f32[64,960]{1,0:T(8,128)}) custom-call(f32[512,128]{1,0:T(8,128)} %get-tuple-element.5.sums_ref, f32[64,128]{1,0:T(8,128)} %get-tuple-element.6.wide_ref, f32[64,2048]{1,0:T(8,128)} %panel_ref.3), custom_call_target="tpu_custom_call" | custom-call | tf_op jit(solution)/shard_map/apply_factor/pallas_call | solution.py:394

commit v7 on v6

--- a/solution.py
+++ b/solution.py
@@ -23,16 +23,18 @@
     return jnp.dot(left, right, preferred_element_type=jnp.float32)
 
 
-def eliminate(gram, out_ref):
+def eliminate(gram, out_ref, mid_ref, begin, end):
     width = gram.shape[0]
     row = lax.broadcasted_iota(jnp.int32, (width, width), 0)
     column = lax.broadcasted_iota(jnp.int32, (width, width), 1)
     wide = jnp.concatenate([gram, jnp.where(row == column, 1.0, 0.0)], axis=1)
     n_groups = width // 8
     sublane = lax.broadcasted_iota(jnp.int32, (8, 2 * width), 0)
+    if begin:
+        wide = mid_ref[...]
     group = [wide[8 * g : 8 * g + 8, :] for g in range(n_groups)]
     step = 4
-    for first in range(0, width, step):
+    for first in range(begin, end, step):
         g0 = first // 8
         live = range(g0, n_groups)
         columns = [
@@ -57,6 +59,9 @@
                 group[g] = group[g] - factor * scaled_row
                 for l in range(k + 1, step):
                     columns[l][g] = columns[l][g] - factor * heads[l - k - 1]
+    if end < width:
+        for g in range(end // 8, n_groups):
+            mid_ref[8 * g : 8 * g + 8, :] = group[g]
 
 
 def write_upper(root_rows, wide_ref, upper_ref):
@@ -113,44 +118,59 @@
     rows_vmem,
     panel_turned,
     part,
+    mid_ref,
     gram_own,
-    gram_gy,
+    gram_pair,
+    gram_chip,
+    gram_plane,
     gram_mid,
-    gram_gx,
+    gram_line,
     half_in,
     half_sum,
+    quarter_in,
+    quarter_sum,
     piece_in,
     total,
     load_panel_sem,
     load_sem,
-    gy_send,
-    gy_recv,
-    gx_send,
-    gx_recv,
-    half_send,
-    half_recv,
-    rs_send,
-    rs_recv,
-    ag_send,
-    ag_recv,
-    back_send,
-    back_recv,
+    pair_sems,
+    gram_plane_sems,
+    gram_line_sems,
+    half_sems,
+    rs_plane_sems,
+    rs_line_sems,
+    ag_line_sems,
+    ag_plane_sems,
+    back_sems,
 ):
     width = panel_ref.shape[0]
     units = rows_vmem.shape[0] // width
     half_batches = rows_vmem.shape[0] // BATCH // 2
     batch_rows = BATCH // LANES * width
     half_rows = half_batches * batch_rows
-    n_chips = n_gx * n_gy // 2
-    piece = half_rows // n_chips
+    n_rings = n_gy // 2
+    n_plane, n_line = 2 * n_rings, n_gx // 2
+    quarter = half_rows // n_plane
+    piece = quarter // n_line
     me_x, me_y = lax.axis_index("gx"), lax.axis_index("gy")
     core = lax.rem(me_y, 2)
     other = 1 - core
-    chip = me_x * (n_gy // 2) + me_y // 2
+    in_plane = lax.rem(me_x, 2) * n_rings + me_y // 2
+    in_line = me_x // 2
     sibling = (me_x, me_y + 1 - 2 * core)
 
-    def chip_device(index):
-        return (index // (n_gy // 2), lax.rem(index, n_gy // 2) * 2 + core)
+    def plane_index(k):
+        return lax.rem(in_plane + k, n_plane)
+
+    def plane_device(k):
+        index = plane_index(k)
+        return (in_line * 2 + index // n_rings, lax.rem(index, n_rings) * 2 + core)
+
+    def line_index(k):
+        return lax.rem(in_line + k, n_line)
+
+    def line_device(k):
+        return (line_index(k) * 2 + lax.rem(me_x, 2), me_y)
 
     load_panel = pltpu.make_async_copy(panel_ref, panel_vmem, load_panel_sem)
     load_panel.start()
@@ -174,17 +194,13 @@
 
     barrier = pltpu.get_barrier_semaphore()
 
-    @pl.loop(1, n_chips)
-    def _(k):
-        pl.semaphore_signal(
-            barrier, inc=1, device_id=chip_device(lax.rem(chip + k, n_chips)), device_id_type=MESH
-        )
-
-    for k in range(1, n_gy, 2):
-        pl.semaphore_signal(
-            barrier, inc=1, device_id=(me_x, lax.rem(me_y + k, n_gy)), device_id_type=MESH
-        )
-    n_signals = n_chips - 1 + n_gy // 2
+    def greet(device):
+        pl.semaphore_signal(barrier, inc=1, device_id=device, device_id_type=MESH)
+
+    greet(sibling)
+    pl.loop(1, n_plane)(lambda k: greet(plane_device(k)))
+    pl.loop(1, n_line)(lambda k: greet(line_device(k)))
+    n_signals = n_plane + n_line - 1
 
     load_panel.wait()
     panel = panel_vmem[...]
@@ -198,68 +214,51 @@
 
     pl.semaphore_wait(barrier, n_signals)
 
-    def gy_copy(k):
+    def remote(source, target, sems, k, device):
         return pltpu.make_async_remote_copy(
-            src_ref=gram_own,
-            dst_ref=gram_gy.at[k - 1],
-            send_sem=gy_send.at[k - 1],
-            recv_sem=gy_recv.at[k - 1],
-            device_id=(me_x, lax.rem(me_y + k, n_gy)),
+            src_ref=source,
+            dst_ref=target,
+            send_sem=sems.at[0, k],
+            recv_sem=sems.at[1, k],
+            device_id=device,
             device_id_type=MESH,
         )
 
-    def gx_copy(k):
-        return pltpu.make_async_remote_copy(
-            src_ref=gram_mid,
-            dst_ref=gram_gx.at[k - 1],
-            send_sem=gx_send.at[k - 1],
-            recv_sem=gx_recv.at[k - 1],
-            device_id=(lax.rem(me_x + k, n_gx), me_y),
-            device_id_type=MESH,
-        )
+    def pair_copy():
+        return remote(gram_own, gram_pair, pair_sems, 0, sibling)
+
+    def gram_plane_copy(k):
+        return remote(gram_chip, gram_plane.at[k - 1], gram_plane_sems, k - 1, plane_device(k))
+
+    def gram_line_copy(k):
+        return remote(gram_mid, gram_line.at[k - 1], gram_line_sems, k - 1, line_device(k))
 
     def half_copy():
-        return pltpu.make_async_remote_copy(
-            src_ref=part.at[pl.ds(other * half_rows, half_rows)],
-            dst_ref=half_in,
-            send_sem=half_send,
-            recv_sem=half_recv,
-            device_id=sibling,
-            device_id_type=MESH,
-        )
-
-    def scatter_copy(k):
-        to = lax.rem(chip + k, n_chips)
-        return pltpu.make_async_remote_copy(
-            src_ref=half_sum.at[pl.ds(to * piece, piece)],
-            dst_ref=piece_in.at[k - 1],
-            send_sem=rs_send.at[k - 1],
-            recv_sem=rs_recv.at[k - 1],
-            device_id=chip_device(to),
-            device_id_type=MESH,
-        )
-
-    own_start = core * half_rows + chip * piece
-
-    def gather_copy(k):
-        return pltpu.make_async_remote_copy(
-            src_ref=total.at[pl.ds(own_start, piece)],
-            dst_ref=total.at[pl.ds(own_start, piece)],
-            send_sem=ag_send.at[k - 1],
-            recv_sem=ag_recv.at[k - 1],
-            device_id=chip_device(lax.rem(chip + k, n_chips)),
-            device_id_type=MESH,
-        )
+        source = part.at[pl.ds(other * half_rows, half_rows)]
+        return remote(source, half_in, half_sems, 0, sibling)
+
+    def scatter_plane_copy(k):
+        source = half_sum.at[pl.ds(plane_index(k) * quarter, quarter)]
+        return remote(source, quarter_in.at[k - 1], rs_plane_sems, k - 1, plane_device(k))
+
+    def scatter_line_copy(k):
+        source = quarter_sum.at[pl.ds(line_index(k) * piece, piece)]
+        return remote(source, piece_in.at[k - 1], rs_line_sems, k - 1, line_device(k))
+
+    own_quarter = core * half_rows + in_plane * quarter
+    own_piece = own_quarter + in_line * piece
+
+    def gather_line_copy(k):
+        block = total.at[pl.ds(own_piece, piece)]
+        return remote(block, block, ag_line_sems, k - 1, line_device(k))
+
+    def gather_plane_copy(k):
+        block = total.at[pl.ds(own_quarter, quarter)]
+        return remote(block, block, ag_plane_sems, k - 1, plane_device(k))
 
     def back_copy():
-        return pltpu.make_async_remote_copy(
-            src_ref=total.at[pl.ds(core * half_rows, half_rows)],
-            dst_ref=total.at[pl.ds(core * half_rows, half_rows)],
-            send_sem=back_send,
-            recv_sem=back_recv,
-            device_id=sibling,
-            device_id_type=MESH,
-        )
+        block = total.at[pl.ds(core * half_rows, half_rows)]
+        return remote(block, block, back_sems, 0, sibling)
 
     def start_all(copy, count):
         pl.loop(1, count)(lambda k: copy(k).start())
@@ -270,7 +269,7 @@
     def sent_all(copy, count):
         pl.loop(1, count)(lambda k: copy(k).wait_send())
 
-    start_all(gy_copy, n_gy)
+    pair_copy().start()
 
     @pl.loop(0, 2 * half_batches)
     def _(step):
@@ -292,34 +291,59 @@
             turned = pair[k * LANES : (k + 1) * LANES].T
             part[pl.ds(index * batch_rows + k * width, width), :] = turned[:width] + turned[width:]
 
+        @pl.when(step == 0)
+        def _():
+            pair_copy().wait_recv()
+            gram_chip[...] = gram_own[...] + gram_pair[...]
+            start_all(gram_plane_copy, n_plane)
+
         @pl.when(step == half_batches - 1)
         def _():
             half_copy().start()
-            receive_all(gy_copy, n_gy)
-            gram_mid[...] = ordered_sum(gram_own, gram_gy, me_y, n_gy)
-            start_all(gx_copy, n_gx)
+
+        @pl.when(step == half_batches)
+        def _():
+            receive_all(gram_plane_copy, n_plane)
+            gram_mid[...] = ordered_sum(gram_chip, gram_plane, in_plane, n_plane)
+            start_all(gram_line_copy, n_line)
 
     half_copy().wait_recv()
     half_sum[...] = part[pl.ds(core * half_rows, half_rows), :] + half_in[...]
-    start_all(scatter_copy, n_chips)
-
-    receive_all(gx_copy, n_gx)
-    packed = ordered_sum(gram_mid, gram_gx, me_x, n_gx)
-    eliminate(jnp.concatenate([packed[:, :width], packed[:, width:]], axis=0), wide_ref)
-
-    receive_all(scatter_copy, n_chips)
-    own = half_sum[pl.ds(chip * piece, piece), :]
-    for k in range(n_chips - 1):
-        own = own + piece_in[k]
-    total[pl.ds(own_start, piece), :] = own
-    start_all(gather_copy, n_chips)
-    sent_all(gy_copy, n_gy)
-    sent_all(gx_copy, n_gx)
+    start_all(scatter_plane_copy, n_plane)
+
+    receive_all(gram_line_copy, n_line)
+    packed = ordered_sum(gram_mid, gram_line, in_line, n_line)
+    gram = jnp.concatenate([packed[:, :width], packed[:, width:]], axis=0)
+    columns = width // 2
+    eliminate(gram, wide_ref, mid_ref, 0, columns)
+
+    receive_all(scatter_plane_copy, n_plane)
+    summed = half_sum[pl.ds(in_plane * quarter, quarter), :]
+    for k in range(n_plane - 1):
+        summed = summed + quarter_in[k]
+    quarter_sum[...] = summed
+    start_all(scatter_line_copy, n_line)
+
+    eliminate(gram, wide_ref, mid_ref, columns, width)
+
+    receive_all(scatter_line_copy, n_line)
+    summed = quarter_sum[pl.ds(in_line * piece, piece), :]
+    for k in range(n_line - 1):
+        summed = summed + piece_in[k]
+    total[pl.ds(own_piece, piece), :] = summed
+    start_all(gather_line_copy, n_line)
+    pair_copy().wait_send()
     half_copy().wait_send()
-    sent_all(scatter_copy, n_chips)
-    receive_all(gather_copy, n_chips)
+    sent_all(gram_plane_copy, n_plane)
+    sent_all(gram_line_copy, n_line)
+    sent_all(scatter_plane_copy, n_plane)
+    sent_all(scatter_line_copy, n_line)
+    receive_all(gather_line_copy, n_line)
+    start_all(gather_plane_copy, n_plane)
+    sent_all(gather_line_copy, n_line)
+    receive_all(gather_plane_copy, n_plane)
     back_copy().start()
-    sent_all(gather_copy, n_chips)
+    sent_all(gather_plane_copy, n_plane)
     back_copy().wait_recv()
     sums_ref[...] = total[...]
     back_copy().wait_send()
@@ -330,8 +354,9 @@
     rows = width + following.shape[0]
     all_rows = rows // LANES * width
     half_rows = all_rows // 2
-    n_chips = n_gx * n_gy // 2
-    piece = half_rows // n_chips
+    n_plane, n_line = n_gy, n_gx // 2
+    quarter = half_rows // n_plane
+    piece = quarter // n_line
     gram_block = (width // 2, 2 * width)
     dma = pltpu.SemaphoreType.DMA
     f32 = jnp.float32
@@ -351,28 +376,30 @@
             pltpu.VMEM((rows, cells), f32),
             pltpu.VMEM((cells, 2 * width), jnp.bfloat16),
             pltpu.VMEM((all_rows, LANES), f32),
+            pltpu.VMEM((width, 2 * width), f32),
             pltpu.VMEM(gram_block, f32),
-            pltpu.VMEM((n_gy - 1,) + gram_block, f32),
             pltpu.VMEM(gram_block, f32),
-            pltpu.VMEM((n_gx - 1,) + gram_block, f32),
+            pltpu.VMEM(gram_block, f32),
+            pltpu.VMEM((n_plane - 1,) + gram_block, f32),
+            pltpu.VMEM(gram_block, f32),
+            pltpu.VMEM((n_line - 1,) + gram_block, f32),
             pltpu.VMEM((half_rows, LANES), f32),
             pltpu.VMEM((half_rows, LANES), f32),
-            pltpu.VMEM((n_chips - 1, piece, LANES), f32),
+            pltpu.VMEM((n_plane - 1, quarter, LANES), f32),
+            pltpu.VMEM((quarter, LANES), f32),
+            pltpu.VMEM((n_line - 1, piece, LANES), f32),
             pltpu.VMEM((all_rows, LANES), f32),
             dma,
             dma((rows // width,)),
-            dma((n_gy - 1,)),
-            dma((n_gy - 1,)),
-            dma((n_gx - 1,)),
-            dma((n_gx - 1,)),
-            dma,
-            dma,
-            dma((n_chips - 1,)),
-            dma((n_chips - 1,)),
-            dma((n_chips - 1,)),
-            dma((n_chips - 1,)),
-            dma,
-            dma,
+            dma((2, 1)),
+            dma((2, n_plane - 1)),
+            dma((2, n_line - 1)),
+            dma((2, 1)),
+            dma((2, n_plane - 1)),
+            dma((2, n_line - 1)),
+            dma((2, n_line - 1)),
+            dma((2, n_plane - 1)),
+            dma((2, 1)),
         ],
         compiler_params=pltpu.CompilerParams(
             collective_id=0, has_side_effects=True, vmem_limit_bytes=56 * 2**20
@@ -417,7 +444,7 @@
     blocks = cross.shape[1] // LANES
     sums = cross.reshape(width, blocks, LANES).transpose(1, 0, 2).reshape(blocks * width, LANES)
     wide = pl.pallas_call(
-        lambda gram_ref, wide_ref: eliminate(gram_ref[...], wide_ref),
+        lambda gram_ref, wide_ref: eliminate(gram_ref[...], wide_ref, None, 0, width),
         out_shape=jax.ShapeDtypeStruct((width, 2 * width), jnp.float32),
         name="factor",
     )(cross[:, -width:])

time: 28.4 us -> 31 us (1.092)
  Pallas kernels: 27.7 us -> 30.2 us
    pallas_call x1, Pallas kernels: 25.3 us -> 27.8 us  [exchanged(): pl.pallas_call(functools.partial(sum_kernel, n_gx, n_gy), out_shape=(jax....]
where the time goes in v7:
time: 31 us; the launch traced here: 30.8 us
  Pallas kernels  30.2 us (97%)
  between operations  0.64 us (2%)
    pallas_call x1, Pallas kernels, exchanged(): pl.pallas_call(functools.partial(sum_kernel, n_gx, n_gy), out_shape=(jax....  27.8 us
    pallas_call x1, Pallas kernels, applied(): pl.pallas_call(functools.partial(apply_kernel, root_rows), out_shape=(jax...  2.4 us

profile of v7, /device:TPU:0, one launch (start us, length us, event | category | flops | bytes accessed | tf_op | source)
XLA Modules:
  0.0 30.8 jit_solution(5155905361173777303)
XLA Ops:
  0.6 27.8 %sum_and_factor.1 = (f32[512,128]{1,0:T(8,128)}, f32[64,128]{1,0:T(8,128)}) custom-call(f32[64,2048]{1,0:T(8,128)} %panel_ref.3, f32[960,2048]{1,0:T(8,128)} %following_ref.1), custom_call_target="tpu_custom_call" | custom-call | tf_op jit(solution)/shard_map/sum_and_factor/pallas_call | solution.py:363
  28.4 2.4 %apply_factor.1 = (f32[64,2048]{1,0:T(8,128)}, f32[64,64]{1,0:T(8,128)}, f32[64,960]{1,0:T(8,128)}) custom-call(f32[512,128]{1,0:T(8,128)} %get-tuple-element.5.sums_ref, f32[64,128]{1,0:T(8,128)} %get-tuple-element.6.wide_ref, f32[64,2048]{1,0:T(8,128)} %panel_ref.3), custom_call_target="tpu_custom_call" | custom-call | tf_op jit(solution)/shard_map/apply_factor/pallas_call | solution.py:421

commit v8 on v6

--- a/solution.py
+++ b/solution.py
@@ -251,12 +251,13 @@
             device_id_type=MESH,
         )
 
-    def back_copy():
-        return pltpu.make_async_remote_copy(
-            src_ref=total.at[pl.ds(core * half_rows, half_rows)],
-            dst_ref=total.at[pl.ds(core * half_rows, half_rows)],
-            send_sem=back_send,
-            recv_sem=back_recv,
+    def back_copy(k):
+        start = core * half_rows + lax.rem(chip - k + n_chips, n_chips) * piece
+        return pltpu.make_async_remote_copy(
+            src_ref=total.at[pl.ds(start, piece)],
+            dst_ref=total.at[pl.ds(start, piece)],
+            send_sem=back_send.at[k],
+            recv_sem=back_recv.at[k],
             device_id=sibling,
             device_id_type=MESH,
         )
@@ -313,16 +314,25 @@
         own = own + piece_in[k]
     total[pl.ds(own_start, piece), :] = own
     start_all(gather_copy, n_chips)
+    back_copy(0).start()
+
+    @pl.loop(1, n_chips)
+    def _(k):
+        gather_copy(k).wait_recv()
+        back_copy(k).start()
+
     sent_all(gy_copy, n_gy)
     sent_all(gx_copy, n_gx)
     half_copy().wait_send()
     sent_all(scatter_copy, n_chips)
-    receive_all(gather_copy, n_chips)
-    back_copy().start()
     sent_all(gather_copy, n_chips)
-    back_copy().wait_recv()
+
+    @pl.loop(0, n_chips)
+    def _(k):
+        back_copy(k).wait_recv()
+        back_copy(k).wait_send()
+
     sums_ref[...] = total[...]
-    back_copy().wait_send()
 
 
 def exchanged(panel, following, n_gx, n_gy):
@@ -371,11 +381,11 @@
             dma((n_chips - 1,)),
             dma((n_chips - 1,)),
             dma((n_chips - 1,)),
-            dma,
-            dma,
+            dma((n_chips,)),
+            dma((n_chips,)),
         ],
         compiler_params=pltpu.CompilerParams(
-            collective_id=0, has_side_effects=True, vmem_limit_bytes=56 * 2**20
+            collective_id=0, has_side_effects=True, vmem_limit_bytes=107 * 2**19
         ),
         name="sum_and_factor",
     )(panel, following)
@@ -398,7 +408,7 @@
             jax.ShapeDtypeStruct((width, width), f32),
             jax.ShapeDtypeStruct((width, next_count), f32),
         ),
-        compiler_params=pltpu.CompilerParams(vmem_limit_bytes=60 * 2**20),
+        compiler_params=pltpu.CompilerParams(vmem_limit_bytes=16 * 2**20),
         name="apply_factor",
     )(sums, wide, panel)
 

time: 28.4 us -> 26.9 us (0.947)
  Pallas kernels: 27.7 us -> 26.1 us
    pallas_call x1, Pallas kernels: 2.4 us -> 1.26 us  [applied(): pl.pallas_call(functools.partial(apply_kernel, root_rows), out_shape=(jax...]
    pallas_call x1, Pallas kernels: 25.3 us -> 24.8 us  [exchanged(): pl.pallas_call(functools.partial(sum_kernel, n_gx, n_gy), out_shape=(jax....]
where the time goes in v8:
time: 26.9 us; the launch traced here: 26.7 us
  Pallas kernels  26.1 us (97%)
  between operations  0.65 us (2%)
    pallas_call x1, Pallas kernels, exchanged(): pl.pallas_call(functools.partial(sum_kernel, n_gx, n_gy), out_shape=(jax....  24.8 us
    pallas_call x1, Pallas kernels, applied(): pl.pallas_call(functools.partial(apply_kernel, root_rows), out_shape=(jax...  1.26 us

profile of v8, /device:TPU:0, one launch (start us, length us, event | category | flops | bytes accessed | tf_op | source)
XLA Modules:
  0.0 26.7 jit_solution(15928488478049396636)
XLA Ops:
  0.6 0.0 copy-start
  0.6 24.8 %sum_and_factor.1 = (f32[512,128]{1,0:T(8,128)S(1)}, f32[64,128]{1,0:T(8,128)S(1)}) custom-call(f32[64,2048]{1,0:T(8,128)} %panel_ref.3, f32[960,2048]{1,0:T(8,128)} %following_ref.1), custom_call_target="tpu_custom_call" | custom-call | tf_op jit(solution)/shard_map/sum_and_factor/pallas_call | solution.py:348
  25.4 0.0 copy-done
  25.4 1.3 %apply_factor.1 = (f32[64,2048]{1,0:T(8,128)}, f32[64,64]{1,0:T(8,128)}, f32[64,960]{1,0:T(8,128)}) custom-call(f32[512,128]{1,0:T(8,128)S(1)} %get-tuple-element.5.sums_ref, f32[64,128]{1,0:T(8,128)S(1)} %get-tuple-element.6.wide_ref, f32[64,2048]{1,0:T(8,128)S(1)} %copy-done), custom_call_target="tpu_custom_call" | custom-call | tf_op jit(solution)/shard_map/apply_factor/pallas_call | solution.py:404
Async XLA Ops:
  0.6 24.8 %copy-start = (f32[64,2048]{1,0:T(8,128)S(1)}, f32[64,2048]{1,0:T(8,128)}, u32[]{:S(2)}) copy-start(f32[64,2048]{1,0:T(8,128)} %panel_ref.3) | copy-start | bytes 1572868

commit v9 on v8

--- a/solution.py
+++ b/solution.py
@@ -265,6 +265,12 @@
     def start_all(copy, count):
         pl.loop(1, count)(lambda k: copy(k).start())
 
+    def turned_order(k):
+        return lax.rem(k + n_chips // 2 - 2, n_chips - 1) + 1
+
+    def far_first(copy):
+        pl.loop(1, n_chips)(lambda k: copy(turned_order(k)).start())
+
     def receive_all(copy, count):
         pl.loop(1, count)(lambda k: copy(k).wait_recv())
 
@@ -302,7 +308,7 @@
 
     half_copy().wait_recv()
     half_sum[...] = part[pl.ds(core * half_rows, half_rows), :] + half_in[...]
-    start_all(scatter_copy, n_chips)
+    far_first(scatter_copy)
 
     receive_all(gx_copy, n_gx)
     packed = ordered_sum(gram_mid, gram_gx, me_x, n_gx)
@@ -313,13 +319,13 @@
     for k in range(n_chips - 1):
         own = own + piece_in[k]
     total[pl.ds(own_start, piece), :] = own
-    start_all(gather_copy, n_chips)
+    far_first(gather_copy)
     back_copy(0).start()
 
     @pl.loop(1, n_chips)
     def _(k):
-        gather_copy(k).wait_recv()
-        back_copy(k).start()
+        gather_copy(turned_order(k)).wait_recv()
+        back_copy(turned_order(k)).start()
 
     sent_all(gy_copy, n_gy)
     sent_all(gx_copy, n_gx)

time: 26.9 us -> 27.2 us (1.011)
  Pallas kernels: 26.1 us -> 26.4 us
    pallas_call x1, Pallas kernels: 24.8 us -> 25.1 us  [exchanged(): pl.pallas_call(functools.partial(sum_kernel, n_gx, n_gy), out_shape=(jax....]
where the time goes in v9:
time: 27.2 us; the launch traced here: 27 us
  Pallas kernels  26.4 us (97%)
  between operations  0.65 us (2%)
    pallas_call x1, Pallas kernels, exchanged(): pl.pallas_call(functools.partial(sum_kernel, n_gx, n_gy), out_shape=(jax....  25.1 us
    pallas_call x1, Pallas kernels, applied(): pl.pallas_call(functools.partial(apply_kernel, root_rows), out_shape=(jax...  1.26 us

profile of v9, /device:TPU:0, one launch (start us, length us, event | category | flops | bytes accessed | tf_op | source)
XLA Modules:
  0.0 27.0 jit_solution(7093200217831495312)
XLA Ops:
  0.6 0.0 copy-start
  0.6 25.1 %sum_and_factor.1 = (f32[512,128]{1,0:T(8,128)S(1)}, f32[64,128]{1,0:T(8,128)S(1)}) custom-call(f32[64,2048]{1,0:T(8,128)} %panel_ref.3, f32[960,2048]{1,0:T(8,128)} %following_ref.1), custom_call_target="tpu_custom_call" | custom-call | tf_op jit(solution)/shard_map/sum_and_factor/pallas_call | solution.py:354
  25.7 0.0 copy-done
  25.8 1.3 %apply_factor.1 = (f32[64,2048]{1,0:T(8,128)}, f32[64,64]{1,0:T(8,128)}, f32[64,960]{1,0:T(8,128)}) custom-call(f32[512,128]{1,0:T(8,128)S(1)} %get-tuple-element.5.sums_ref, f32[64,128]{1,0:T(8,128)S(1)} %get-tuple-element.6.wide_ref, f32[64,2048]{1,0:T(8,128)S(1)} %copy-done), custom_call_target="tpu_custom_call" | custom-call | tf_op jit(solution)/shard_map/apply_factor/pallas_call | solution.py:410
Async XLA Ops:
  0.6 25.1 %copy-start = (f32[64,2048]{1,0:T(8,128)S(1)}, f32[64,2048]{1,0:T(8,128)}, u32[]{:S(2)}) copy-start(f32[64,2048]{1,0:T(8,128)} %panel_ref.3) | copy-start | bytes 1572868
